TPU v7x, 32 devices: a whole 2x2x4 slice. The times are simulated.
32 devices in a mesh: groups: 2 (over x), row: 4 (over y, core), col: 4 (over z).
Axes of the slice: x: 2, y: 2, z: 4, core: 2. Of those that a mesh axis runs over, the one named last changes fastest.
Arguments:
- zroot: float32 [4096, 2048], P(('groups', 'row')), parts along dimension 0, as said below
- panel_one: float32 [8, 2048, 1024], P(('groups', 'col'), 'row'), parts along dimension 0, may hold values from -0.125 to 0.125
- inv_one: float32 [8, 1024, 1024], P(('groups', 'col')), parts along dimension 0
- panel_two_j: float32 [16, 1024, 512], P(('groups', 'col'), 'row'), parts along dimension 0, may hold values from -0.109375 to 0.109375
- panel_two_r: float32 [16, 2048, 512], P(('groups', 'col'), 'row'), parts along dimension 0, may hold values from -0.109375 to 0.109375
- inv_two: float32 [16, 512, 512], P(('groups', 'col')), parts along dimension 0
- parents: int32 [16], P(('groups', 'col')), parts along dimension 0, may hold values from 0 to 3
- widths: int32 [16], P(('groups', 'col')), parts along dimension 0, may hold values from 256 to 512, as said below
- pattern_j: int32 [16, 16], P(('groups', 'col'), 'row'), parts along dimension 0, may hold values 0 or 1
- pattern_r: int32 [16, 32], P(('groups', 'col'), 'row'), parts along dimension 0, may hold values 0 or 1
Outputs:
- var_one: float32 [8, 1024], P(('groups', 'col'), 'row'), parts along dimension 0
- var_two: float32 [16, 512], P(('groups', 'col'), 'row'), parts along dimension 0
- z_two_j: float32 [16, 1024, 512], P(('groups', 'col'), 'row'), parts along dimension 0
- z_two_r: float32 [16, 2048, 512], P(('groups', 'col'), 'row'), parts along dimension 0
There are 2 independent parts, one for each index of `groups`. A program takes and returns all parts, laid end to end along the dimension named above; each array names one. Nothing has to cross between parts.
Inputs may be any that keep to these rules, and one draw needn't show every extreme that they name: zroot is symmetric: it equals its transpose up to rounding, as a selected inverse block of a symmetric matrix does. `widths`: the live width of each level-2 supernode; columns at or past it are padding. `parents`: index of the level-1 parent of each level-2 supernode. `pattern_j`: 1 where a tile of 64 rows of the panel is stored. `pattern_r`: 1 where a tile of 64 rows of the panel is stored.
All inputs are finite; a program needn't handle non-finite values. No bound on the sum of `pattern_j` or of `pattern_r` on one device may be relied on, other than what follows from the above.
Results may differ from a plain program's by a relative error of at most 0.0003.
Values sent between devices are 32-bit elements; how exact they have to be, the bound alone decides.
A program may use at most 128 MiB of HBM per device.

v0:
```python
import jax
import jax.numpy as jnp
from jax import lax
from jax.sharding import PartitionSpec as P

TILE = 64


def product(left, right):
    return jnp.dot(left, right, precision=lax.Precision.HIGHEST, preferred_element_type=jnp.float32)


def batched(form, left, right):
    return jnp.einsum(
        form, left, right, precision=lax.Precision.HIGHEST, preferred_element_type=jnp.float32
    )


def body(
    zroot,
    panel_one,
    inv_one,
    panel_two_j,
    panel_two_r,
    inv_two,
    parents,
    widths,
    pattern_j,
    pattern_r,
):
    root_rows = zroot.shape[0]
    inverse = inv_one[0]
    width_one = inverse.shape[0]
    node_rows = width_one // lax.axis_size("row")
    node_start = lax.axis_index("row") * node_rows
    factor = product(panel_one[0], inverse)
    columns = zroot
    root_block = lax.psum_scatter(
        -product(columns.T, factor), "row", scatter_dimension=0, tiled=True
    )
    own_columns = lax.dynamic_slice_in_dim(inverse, node_start, node_rows, 1)
    columns = factor
    diagonal_block = product(own_columns.T, inverse) + lax.psum_scatter(
        -product(columns.T, root_block), "row", scatter_dimension=0, tiled=True
    )
    var_one = jnp.diagonal(lax.dynamic_slice_in_dim(diagonal_block, node_start, node_rows, 1))[
        None, :
    ]
    flipped = lax.all_to_all(root_block, "row", split_axis=1, concat_axis=0, tiled=True).T
    fetched = (
        lax.all_gather(diagonal_block[None], "col", axis=0, tiled=True),
        lax.all_gather(flipped[None], "col", axis=0, tiled=True),
        lax.all_gather(root_block[None], "col", axis=0, tiled=True),
    )
    parent_jj = jnp.take(fetched[0], parents, axis=0)
    parent_jr = jnp.take(fetched[1], parents, axis=0)
    parent_rj = jnp.take(fetched[2], parents, axis=0)
    nodes = inv_two.shape[0]
    width_two = inv_two.shape[1]
    live = (jnp.arange(width_two)[None, :] < widths[:, None]).astype(jnp.float32)
    mask_j = jnp.repeat(pattern_j.astype(jnp.float32), TILE, axis=1)
    mask_r = jnp.repeat(pattern_r.astype(jnp.float32), TILE, axis=1)
    masked_j = panel_two_j * mask_j[:, :, None] * live[:, None, :]
    masked_r = panel_two_r * mask_r[:, :, None] * live[:, None, :]
    factor_j = batched("nak,nkm->nam", masked_j, inv_two)
    factor_r = batched("nak,nkm->nam", masked_r, inv_two)
    stacked_rows = node_rows + root_rows
    blocks_in = lax.axis_size("row") * stacked_rows // stacked_rows
    upper = -(
        batched("nab,nam->bnm", parent_jj, factor_j) + batched("nab,nam->bnm", parent_rj, factor_r)
    )
    lower = -(
        batched("nab,nam->bnm", parent_jr, factor_j) + batched("ab,nam->bnm", zroot, factor_r)
    )
    upper = upper.reshape(blocks_in, node_rows, nodes, width_two)
    lower = lower.reshape(blocks_in, root_rows, nodes, width_two)
    ancestors = lax.psum_scatter(
        jnp.concatenate([upper, lower], axis=1).reshape(
            lax.axis_size("row") * stacked_rows, nodes, width_two
        ),
        "row",
        scatter_dimension=0,
        tiled=True,
    )
    block_j = jnp.transpose(ancestors[:node_rows], (1, 0, 2))
    block_r = jnp.transpose(ancestors[node_rows:], (1, 0, 2))
    partial_terms = -(jnp.sum(factor_j * block_j, axis=1) + jnp.sum(factor_r * block_r, axis=1))
    summed = lax.psum_scatter(partial_terms, "row", scatter_dimension=1, tiled=True)
    share = summed.shape[1]
    column_start = lax.axis_index("row") * share
    squares = jnp.sum(inv_two * inv_two, axis=1)
    live_share = lax.dynamic_slice_in_dim(live, column_start, share, 1)
    square_share = lax.dynamic_slice_in_dim(squares, column_start, share, 1)
    var_two = live_share * (square_share + summed)
    return (var_one, var_two, block_j, block_r)


def solution(mesh):
    return jax.shard_map(
        body,
        mesh=mesh,
        in_specs=(
            P(("groups", "row"), None),
            P(("groups", "col"), "row", None),
            P(("groups", "col"), None, None),
            P(("groups", "col"), "row", None),
            P(("groups", "col"), "row", None),
            P(("groups", "col"), None, None),
            P(("groups", "col")),
            P(("groups", "col")),
            P(("groups", "col"), "row"),
            P(("groups", "col"), "row"),
        ),
        out_specs=(
            P(("groups", "col"), "row"),
            P(("groups", "col"), "row"),
            P(("groups", "col"), "row", None),
            P(("groups", "col"), "row", None),
        ),
        check_vma=False,
    )
```

profile of v0, /device:TPU:0, one launch (start us, length us, event | category | flops | bytes accessed | tf_op | source)
XLA Modules:
  0.0 723.6 jit_solution(11869703640551701223)
XLA Ops:
  7.2 1.5 copy-done
  8.8 9.1 %fusion.2 = f32[512,1024]{1,0:T(8,128)S(1)} fusion(f32[1,1024,1024]{2,1,0:T(8,128)} %param.12, f32[1,512,1024]{2,1,0:T(8,128)S(1)} %copy-done), kind=kOutput, calls=%fused_computation.9 | convolution fusion | flops 6442450944 | bytes 8388608 | tf_op jit(solution)/shard_map/dot_general | solution.py:10
  17.9 1.3 copy-done.3
  19.2 15.7 %negate_bitcast_fusion.1 = f32[2048,1024]{0,1:T(8,128)} fusion(f32[512,1024]{1,0:T(8,128)S(1)} %fusion.2, f32[512,2048]{1,0:T(8,128)S(1)} %copy-done.9), kind=kOutput, calls=%fused_computation.6 | convolution fusion | flops 12886999040 | bytes 14680064 | tf_op jit(solution)/shard_map/dot_general | solution.py:10
  35.0 11.6 %reduce-scatter.9.cloned.1.call-start = ((), (), s32[]{:S(2)}) async-start(), calls=%async_computation.6 | async-start | bytes 5242880 | tf_op jit(solution)/shard_map/reduce_scatter | solution.py:43
  46.5 63.0 %reduce-scatter.7.cloned.1.call-done = f32[512,1024]{0,1:T(8,128)} async-done(((f32[2048,1024]{0,1:T(8,128)}), f32[512,1024]{0,1:T(8,128)}) %reduce-scatter.7.cloned.1.call-update) | async-done | bytes 2097168 | tf_op jit(solution)/shard_map/reduce_scatter | solution.py:38
  109.6 16.0 %convolution_negate_fusion = f32[1024,1024]{1,0:T(8,128)} fusion(f32[512,1024]{1,0:T(8,128)S(1)} %copy-done.4, f32[512,1024]{0,1:T(8,128)} %reduce-scatter.7.cloned.1.call-done), kind=kOutput, calls=%fused_computation.17 | convolution fusion | flops 6443499520 | bytes 8388608 | tf_op jit(solution)/shard_map/dot_general | solution.py:10
  125.6 0.7 all-gather.9.cloned.1.call-update
  126.3 0.8 copy-done.8
  127.1 1.8 copy.32
  128.9 42.8 %all_to_all.19 = f32[512,4,256]{2,0,1:T(8,128)} all-to-all(f32[512,4,256]{2,0,1:T(8,128)} %copy.32), channel_id=1, replica_groups=mesh['groups'=2,'row'=4,'col'=4] {'row'}, dimensions={1} | all-to-all | bytes 4194304 | tf_op jit(solution)/shard_map/all_to_all | solution.py:49
  171.8 0.0 all-gather.7.cloned.1.call-start
  171.9 10.9 %reduce-scatter.9.cloned.1.call-done = f32[256,1024]{1,0:T(8,128)} async-done(((f32[1024,1024]{1,0:T(8,128)}), f32[256,1024]{1,0:T(8,128)}) %reduce-scatter.9.cloned.1.call-update) | async-done | bytes 1048592 | tf_op jit(solution)/shard_map/reduce_scatter | solution.py:43
  182.8 7.4 %fusion.18 = f32[256,1024]{1,0:T(8,128)} fusion(f32[256,1024]{1,0:T(8,128)} %reduce-scatter.9.cloned.1.call-done, f32[1,1024,1024]{2,1,0:T(8,128)} %param.12, s32[]{:T(128)S(6)} %select_n.33), kind=kOutput, calls=%fused_computation.30 | convolution fusion | flops 3221487616 | bytes 7340036 | tf_op jit(solution)/shard_map/dot_general | solution.py:10
  190.3 0.0 reduce-scatter.11.cloned.1.call-start
  190.4 0.1 broadcast_in_dim.59
  190.4 0.1 mul.57
  190.5 0.1 broadcast_in_dim.64
  190.6 0.1 mul.62
  190.7 0.1 compare_convert_fusion
  190.8 3.5 fusion.25
  194.3 3.6 fusion.12
  198.0 16.0 %fusion = f32[2,512,2048]{2,1,0:T(8,128)} fusion(f32[2,512,512]{2,1,0:T(8,128)S(1)} %fusion.12, f32[512,2048]{1,0:T(8,128)S(1)} %copy-done.10), kind=kOutput, calls=%fused_computation.7 | convolution fusion | flops 12884901888 | bytes 14680064 | tf_op jit(solution)/shard_map/ab,nam->bnm/dot_general | solution.py:14
  214.0 120.1 %all-gather.9.cloned.1.call-done = f32[2048,1024]{0,1:T(8,128)} async-done(((f32[512,1024]{0,1:T(8,128)}), f32[2048,1024]{0,1:T(8,128)}) %all-gather.9.cloned.1.call-update) | async-done | bytes 8388624 | tf_op jit(solution)/shard_map/all_gather | solution.py:53
  334.2 9.4 %copy.42 = f32[2048,1024]{1,0:T(8,128)} copy(f32[2048,1024]{0,1:T(8,128)} %all-gather.9.cloned.1.call-done) | data formatting | bytes 16777216 | tf_op jit(solution)/shard_map/all_gather | solution.py:53
  343.5 6.8 gather_fusion.2
  350.3 10.2 %fusion.7 = f32[2,512,1024]{2,1,0:T(8,128)} fusion(f32[2,512,512]{2,1,0:T(8,128)S(1)} %fusion.12, f32[2,512,1024]{2,1,0:T(8,128)} %gather_fusion.2, pred[2]{0:T(512)(128)(4,1)S(1)} %compare_and_fusion), kind=kOutput, calls=%fused_computation.15 | convolution fusion | flops 6443499520 | bytes 10485762 | tf_op jit(solution)/shard_map/nab,nam->bnm/dot_general | solution.py:14
  360.5 122.9 %all-gather.11.cloned.1.call-done = f32[1024,2048]{0,1:T(8,128)} async-done(((f32[256,2048]{0,1:T(8,128)}), f32[1024,2048]{0,1:T(8,128)}) %all-gather.11.cloned.1.call-update) | async-done | bytes 8388624 | tf_op jit(solution)/shard_map/all_gather | solution.py:52
  483.4 9.4 %copy.33 = f32[1024,2048]{1,0:T(8,128)} copy(f32[1024,2048]{0,1:T(8,128)} %all-gather.11.cloned.1.call-done) | data formatting | bytes 16777216 | tf_op jit(solution)/shard_map/all_gather | solution.py:52
  492.8 6.2 gather_fusion.3
  499.1 13.6 %negate_bitcast_fusion = f32[2048,2,512]{0,2,1:T(8,128)} fusion(f32[2,512,2048]{2,1,0:T(8,128)} %fusion, f32[2,256,512]{2,1,0:T(8,128)S(1)} %fusion.25, f32[2,256,2048]{2,1,0:T(8,128)} %gather_fusion.3, pred[2]{0:T(512)(128)(4,1)S(1)} %compare_and_fusion), kind=kOutput, calls=%fused_computation.5 | convolution fusion | flops 6447693824 | bytes 22020098 | tf_op jit(solution)/shard_map/nab,nam->bnm/dot_general | solution.py:14
  512.7 8.7 %copy.44 = f32[2048,2,512]{2,0,1:T(8,128)} copy(f32[2048,2,512]{0,2,1:T(8,128)} %negate_bitcast_fusion) | data formatting | bytes 16777216 | tf_op jit(solution)/shard_map/reshape | solution.py:76
  521.4 42.4 %all-gather.7.cloned.1.call-done = f32[1024,1024]{1,0:T(8,128)} async-done(((f32[256,1024]{1,0:T(8,128)}), f32[1024,1024]{1,0:T(8,128)}) %all-gather.7.cloned.1.call-update) | async-done | bytes 4194320 | tf_op jit(solution)/shard_map/all_gather | solution.py:51
  563.9 2.9 gather_fusion.1
  566.7 7.0 negate_bitcast_fusion.2
  573.7 5.4 copy.43
  579.1 10.6 %pad_maximum_fusion = f32[4,768,2,512]{3,1,0,2:T(8,128)} fusion(f32[4,512,2,512]{3,1,0,2:T(8,128)} %bitcast.55, f32[4,256,2,512]{3,1,0,2:T(8,128)} %bitcast.59), kind=kLoop, calls=%fused_computation.4 | loop fusion | flops 3145728 | bytes 25165824 | tf_op jit(solution)/shard_map/concatenate | solution.py:78
  589.8 1.5 copy-done.7
  591.3 0.2 multiply_reduce_fusion.1
  591.5 96.0 %reduce-scatter.11.cloned.1.call-done = f32[768,2,512]{2,0,1:T(8,128)} async-done(((f32[3072,2,512]{2,0,1:T(8,128)}), f32[768,2,512]{2,0,1:T(8,128)}) %reduce-scatter.11.cloned.1.call-update) | async-done | bytes 3145744 | tf_op jit(solution)/shard_map/reduce_scatter | solution.py:77
  687.5 4.1 multiply_reduce_fusion
  691.6 2.4 multiply_reduce_fusion.2
  694.0 0.9 copy.45
  694.9 1.0 constant_dynamic-slice_fusion
  695.9 2.9 gather_fusion
  698.8 16.3 %reduce-scatter.13.cloned.1.call-done = f32[128,2]{1,0:T(8,128)} async-done(((f32[512,2]{1,0:T(8,128)}), f32[128,2]{1,0:T(8,128)}) %reduce-scatter.13.cloned.1.call-update) | async-done | bytes 1040
  715.1 0.9 copy.46
  716.0 0.6 add_multiply_fusion
  (45 shorter events, 0.4 us)
Async XLA Ops:
  7.2 1.6 copy-start
  7.2 102.4 %reduce-scatter.7.cloned.1.call-start = ((), (), s32[]{:S(2)}) async-start(), calls=%async_computation.5 | async-start | bytes 10485760 | tf_op jit(solution)/shard_map/reduce_scatter | solution.py:38
  8.8 10.5 %copy-start.9 = (f32[512,2048]{1,0:T(8,128)S(1)}, f32[512,2048]{1,0:T(8,128)}, u32[]{:S(2)}) copy-start(f32[512,2048]{1,0:T(8,128)} %param.10) | copy-start | bytes 12582916
  17.9 1.3 copy-start.3
  34.9 74.6 %copy-start.4 = (f32[512,1024]{1,0:T(8,128)S(1)}, f32[512,1024]{1,0:T(8,128)}, u32[]{:S(2)}) copy-start(f32[512,1024]{1,0:T(8,128)} %copy-done.3) | copy-start | bytes 6291460
  35.0 147.9 %reduce-scatter.9.cloned.1.call-start = ((), (), s32[]{:S(2)}) async-start(), calls=%async_computation.6 | async-start | bytes 5242880 | tf_op jit(solution)/shard_map/reduce_scatter | solution.py:43
  125.5 1.6 copy-start.8
  125.5 208.6 %all-gather.9.cloned.1.call-start = ((), (), s32[]{:S(2)}) async-start(), calls=%async_computation.9 | async-start | bytes 10485760 | tf_op jit(solution)/shard_map/all_gather | solution.py:53
  126.3 357.2 %all-gather.11.cloned.1.call-start = ((), (), s32[]{:S(2)}) async-start(), calls=%async_computation.10 | async-start | bytes 10485760 | tf_op jit(solution)/shard_map/all_gather | solution.py:52
  171.8 18.5 %copy-start.12 = (s32[2,4]{1,0:T(2,128)S(1)}, s32[2,4]{1,0:T(2,128)}, u32[]{:S(2)}) copy-start(s32[2,4]{1,0:T(2,128)} %param.18) | copy-start | bytes 100
  171.8 18.5 %copy-start.13 = (s32[2,8]{1,0:T(2,128)S(1)}, s32[2,8]{1,0:T(2,128)}, u32[]{:S(2)}) copy-start(s32[2,8]{1,0:T(2,128)} %param.19) | copy-start | bytes 196
  171.8 18.9 %copy-start.15 = (s32[2]{0:T(128)S(1)}, s32[2]{0:T(128)}, u32[]{:S(2)}) copy-start(s32[2]{0:T(128)} %param.16) | copy-start | bytes 28
  171.8 18.9 %copy-start.14 = (s32[2]{0:T(128)S(1)}, s32[2]{0:T(128)}, u32[]{:S(2)}) copy-start(s32[2]{0:T(128)} %param.17) | copy-start | bytes 28
  171.8 19.0 %copy-start.5 = (f32[2,512,512]{2,1,0:T(8,128)S(1)}, f32[2,512,512]{2,1,0:T(8,128)}, u32[]{:S(2)}) copy-start(f32[2,512,512]{2,1,0:T(8,128)} %param.15) | copy-start | bytes 6291460
  171.8 392.0 %all-gather.7.cloned.1.call-start = ((), (), s32[]{:S(2)}) async-start(), calls=%async_computation.8 | async-start | bytes 5242880 | tf_op jit(solution)/shard_map/all_gather | solution.py:51
  190.3 497.2 %reduce-scatter.11.cloned.1.call-start = ((), (), s32[]{:S(2)}) async-start(), calls=%async_computation.7 | async-start | bytes 15728640 | tf_op jit(solution)/shard_map/reduce_scatter | solution.py:77
  190.7 3.6 copy-start.6
  190.7 3.7 copy-start.11
  194.3 3.7 copy-start.10
  198.0 152.4 %copy-start.2 = (f32[2,512,512]{2,1,0:T(8,128)}, f32[2,512,512]{2,1,0:T(8,128)S(1)}, u32[]{:S(2)}) copy-start(f32[2,512,512]{2,1,0:T(8,128)S(1)} %fusion.12) | copy-start | bytes 6291460
  589.7 1.6 copy-start.7
  589.8 125.4 %reduce-scatter.13.cloned.1.call-start = ((), (), s32[]{:S(2)}) async-start(), calls=%async_computation.11 | async-start | bytes 327680
  687.5 29.1 %copy-start.1 = (f32[1,512,1024]{2,1,0:T(8,128)S(1)}, f32[1,512,1024]{2,1,0:T(8,128)}, u32[]{:S(2)}) copy-start(f32[1,512,1024]{2,1,0:T(8,128)} %param.11) | copy-start | bytes 6291460
Sparse Core Ops, SparseCore 0:
  35.1 74.4 reduce-scatter.6
  125.7 57.1 reduce-scatter.8
  184.4 149.6 all-gather.8
  335.6 147.8 all-gather.10
  484.9 78.9 all-gather.6
  589.9 97.5 reduce-scatter.10
  695.0 20.0 reduce-scatter.12
where the time goes:
time: 732 us; the launch traced here: 724 us
  waiting for transfers between devices  473 us (65%)
  matrix products  102 us (14%)
  local copies, waits for them, and re-layouts  61.8 us (8%)
  blocking collectives  42.8 us (6%)
  other arithmetic  18 us (2%)
  between operations  14.5 us (2%)
  starting transfers between devices  11.8 us (2%)
    all_gather x1, waiting for transfers between devices, body(): lax.all_gather(flipped[None], 'col', axis=0, tiled=True)  123 us
    all_gather x1, waiting for transfers between devices, body(): lax.all_gather(root_block[None], 'col', axis=0, tiled=True)  120 us
    reduce_scatter x1, waiting for transfers between devices, body(): lax.psum_scatter(jnp.concatenate([upper, lower], axis=1).reshape(lax.axis...  96 us
    reduce_scatter x1, waiting for transfers between devices, body(): lax.psum_scatter(-product(columns.T, factor), 'row', scatter_dimension=0,...  63 us
    dot_general x6, matrix products, batched(): jnp.einsum(form, left, right, precision=lax.Precision.HIGHEST, preferred_...  53.9 us
    dot_general x4, matrix products, product(): jnp.dot(left, right, precision=lax.Precision.HIGHEST, preferred_element_t...  48.2 us
    all_to_all x1, blocking collectives, body(): lax.all_to_all(root_block, 'row', split_axis=1, concat_axis=0, tiled=True)  42.8 us
    all_gather x1, waiting for transfers between devices, body(): lax.all_gather(diagonal_block[None], 'col', axis=0, tiled=True)  42.4 us
  transfers between devices with their start and end apart: 7, of which 7 were waited for; matrix products, arithmetic and copies ran while one was open for 14% of the time, Pallas kernels for 0%

commit v1 on v0

v1 whole, which is shorter than its diff:
```python
import jax
import jax.numpy as jnp
from jax import lax
from jax.sharding import PartitionSpec as P

TILE = 64
PRECISION = lax.Precision.HIGH


def product(left, right):
    return jnp.dot(left, right, precision=PRECISION, preferred_element_type=jnp.float32)


def crossed(left, right):
    return lax.dot_general(
        left, right, (((0,), (0,)), ((), ())), precision=PRECISION, preferred_element_type=jnp.float32
    )


def swap(block, bit):
    n = lax.axis_size("row")
    return lax.ppermute(block, "row", [(i, i ^ bit) for i in range(n)])


def own_first(array, axis):
    n = lax.axis_size("row")
    me = lax.axis_index("row")
    share = array.shape[axis] // n
    pieces = [
        lax.dynamic_slice_in_dim(array, (me ^ d) * share, share, axis) for d in range(n)
    ]
    return jnp.concatenate(pieces, axis)


def row_blocks(block):
    n = lax.axis_size("row")
    held = {0: block}
    bit = n // 2
    while bit:
        for d in sorted(held):
            held[d | bit] = swap(held[d], bit)
        bit //= 2
    return [held[d] for d in range(n)]


def row_sum(pieces):
    n = lax.axis_size("row")
    held = dict(enumerate(pieces))
    bit = 1
    while bit < n:
        for d in [d for d in sorted(held) if not d & bit]:
            held[d] = held[d] + swap(held.pop(d | bit), bit)
        bit *= 2
    return held[0]


def reordered(block, d):
    n = lax.axis_size("row")
    share = block.shape[1] // n
    return jnp.concatenate(
        [block[:, (d ^ e) * share : ((d ^ e) + 1) * share] for e in range(n)], 1
    )


def body(
    zroot,
    panel_one,
    inv_one,
    panel_two_j,
    panel_two_r,
    inv_two,
    parents,
    widths,
    pattern_j,
    pattern_r,
):
    n = lax.axis_size("row")
    width_one = inv_one.shape[1]
    node_rows = width_one // n
    nodes, width_two = inv_two.shape[:2]
    root_rows = zroot.shape[0]

    inverse = own_first(inv_one[0], 1)
    factor = product(panel_one[0], inverse)
    all_factors = lax.all_gather(factor, "col", axis=0)
    gram = crossed(inverse[:, :node_rows], inverse)
    factor_tied, gram = lax.optimization_barrier((factor, gram))
    all_grams = lax.all_gather(gram, "col", axis=0)

    live = (jnp.arange(width_two)[None, :] < widths[:, None]).astype(jnp.float32)
    mask_j = jnp.repeat(pattern_j.astype(jnp.float32), TILE, axis=1)
    mask_r = jnp.repeat(pattern_r.astype(jnp.float32), TILE, axis=1)
    factor_j = []
    factor_r = []
    for i in range(nodes):
        masked_j = panel_two_j[i] * mask_j[i][:, None] * live[i][None, :]
        masked_r = panel_two_r[i] * mask_r[i][:, None] * live[i][None, :]
        factor_j.append(product(masked_j, inv_two[i]))
        factor_r.append(product(masked_r, inv_two[i]))
    near_j = jnp.concatenate(factor_j, 1)
    full_j = jnp.concatenate(row_blocks(near_j), 0)

    root = own_first(zroot, 1)
    full_factor = jnp.concatenate(
        [reordered(block, d) for d, block in enumerate(row_blocks(factor))], 0
    )
    image = product(root, full_factor)
    terms = jnp.sum(factor * image, axis=0).reshape(n, node_rows)
    own_squares = jnp.sum(inverse[:, :node_rows] ** 2, axis=0)
    var_one = (own_squares + row_sum([terms[d] for d in range(n)]))[None, :]

    parent_factor = [
        lax.dynamic_index_in_dim(all_factors, parents[i], 0, False) for i in range(nodes)
    ]
    reduced = [
        factor_r[i] - product(parent_factor[i], full_j[:, i * width_two : (i + 1) * width_two])
        for i in range(nodes)
    ]
    block_r = []
    sums_j = []
    for i in range(nodes):
        block_r.append(-product(root, jnp.concatenate(row_blocks(reduced[i]), 0)))
        upper = crossed(parent_factor[i], block_r[i]).reshape(n, node_rows, width_two)
        sums_j.append(row_sum([upper[d] for d in range(n)]))
    block_j = []
    for i in range(nodes):
        parent_gram = lax.dynamic_index_in_dim(all_grams, parents[i], 0, False)
        near = product(parent_gram, full_j[:, i * width_two : (i + 1) * width_two])
        block_j.append(-(near + sums_j[i]))

    corrections = jnp.stack(
        [
            jnp.sum(factor_j[i] * block_j[i], axis=0) + jnp.sum(factor_r[i] * block_r[i], axis=0)
            for i in range(nodes)
        ]
    )
    share = width_two // n
    me = lax.axis_index("row")
    ordered = own_first(corrections, 1).reshape(nodes, n, share)
    summed = row_sum([ordered[:, d] for d in range(n)])
    squares = jnp.sum(inv_two * inv_two, axis=1)
    live_share = lax.dynamic_slice_in_dim(live, me * share, share, 1)
    square_share = lax.dynamic_slice_in_dim(squares, me * share, share, 1)
    var_two = live_share * (square_share - summed)
    return (var_one, var_two, jnp.stack(block_j), jnp.stack(block_r))


def solution(mesh):
    return jax.shard_map(
        body,
        mesh=mesh,
        in_specs=(
            P(("groups", "row"), None),
            P(("groups", "col"), "row", None),
            P(("groups", "col"), None, None),
            P(("groups", "col"), "row", None),
            P(("groups", "col"), "row", None),
            P(("groups", "col"), None, None),
            P(("groups", "col")),
            P(("groups", "col")),
            P(("groups", "col"), "row"),
            P(("groups", "col"), "row"),
        ),
        out_specs=(
            P(("groups", "col"), "row"),
            P(("groups", "col"), "row"),
            P(("groups", "col"), "row", None),
            P(("groups", "col"), "row", None),
        ),
        check_vma=False,
    )
```

time: 732 us -> 289 us (0.39); the launches traced: 724 us -> 289 us
  waiting for transfers between devices: 473 us -> 149 us
  blocking collectives: 42.8 us -> 0 us
  local copies, waits for them, and re-layouts: 61.8 us -> 21 us
  matrix products: 102 us -> 72.9 us
    all_gather x3 -> x2, waiting for transfers between devices: 285 us -> 62.1 us  [the longest x1 62.1 us: body(): all_factors = lax.all_gather(factor, 'col', axis=0)]
    reduce_scatter x3 -> x0, waiting for transfers between devices: 170 us -> none  [the longest x1 96 us: body(): lax.psum_scatter(jnp.concatenate([upper, lower], axis=1).reshape(lax.axis...]
    ppermute x0 -> x24, waiting for transfers between devices: none -> 87.3 us  [swap(): return lax.ppermute(block, 'row', [(i, i ^ bit) for i in range(n)])]
    all_to_all x1 -> x0, blocking collectives: 42.8 us -> none  [body(): lax.all_to_all(root_block, 'row', split_axis=1, concat_axis=0, tiled=True)]
    dot_general x10 -> x15, matrix products: 102 us -> 72.9 us  [the longest x12 59.2 us: product(): jnp.dot(left, right, precision=PRECISION, preferred_element_type=jnp.floa...]
    gather x4 -> x0, local copies, waits for them, and re-layouts: 18.8 us -> none  [the longest x1 6.82 us: body(): parent_rj = jnp.take(fetched[2], parents, axis=0)]
    all_gather x2 -> x0, local copies, waits for them, and re-layouts: 18.7 us -> none  [the longest x1 9.39 us: body(): lax.all_gather(flipped[None], 'col', axis=0, tiled=True)]
    unnamed x8 -> x2, waiting for transfers between devices: 17.1 us -> 0.03 us
  transfers between devices with their start and end apart: 7 -> 26, of which waited for: 7 -> 7; matrix products, arithmetic and copies ran while one was open for 14% -> 32% of each run, Pallas kernels for 0% -> 0%
where the time goes in v1:
time: 289 us
  waiting for transfers between devices  149 us (52%)
  matrix products  72.9 us (25%)
  local copies, waits for them, and re-layouts  21 us (7%)
  between operations  18.4 us (6%)
  starting transfers between devices  14.1 us (5%)
  other arithmetic  12.9 us (4%)
    ppermute x24, waiting for transfers between devices, swap(): return lax.ppermute(block, 'row', [(i, i ^ bit) for i in range(n)])  87.3 us
    all_gather x1, waiting for transfers between devices, body(): all_factors = lax.all_gather(factor, 'col', axis=0)  62.1 us
    dot_general x12, matrix products, product(): jnp.dot(left, right, precision=PRECISION, preferred_element_type=jnp.floa...  59.2 us
    ppermute x24, starting transfers between devices, swap(): return lax.ppermute(block, 'row', [(i, i ^ bit) for i in range(n)])  13.9 us
    dot_general x3, matrix products, crossed(): lax.dot_general(left, right, (((0,), (0,)), ((), ())), precision=PRECISIO...  13.8 us
    slice x3, local copies, waits for them, and re-layouts, reordered(): block[:, (d ^ e) * share:((d ^ e) + 1) * share]  9.28 us
    dynamic_slice x2, local copies, waits for them, and re-layouts, own_first(): lax.dynamic_slice_in_dim(array, (me ^ d) * share, share, axis)  6.9 us
  transfers between devices with their start and end apart: 26, of which 7 were waited for; matrix products, arithmetic and copies ran while one was open for 32% of the time, Pallas kernels for 0%

profile of v1, /device:TPU:0, one launch (start us, length us, event | category | flops | bytes accessed | tf_op | source)
XLA Modules:
  0.0 288.8 jit_solution(17674615914667572050)
XLA Ops:
  7.2 1.5 multiply_reduce_fusion.4
  8.8 2.5 dynamic-slice_bitcast_fusion.2
  11.3 0.9 copy-done.20
  12.9 4.8 %fusion.59 = f32[512,1024]{1,0:T(8,128)} fusion(f32[1,512,1024]{2,1,0:T(8,128)S(1)} %copy-done, f32[1024,256]{1,0:T(8,128)S(1)} %get-tuple-element.13, f32[1024,256]{1,0:T(8,128)S(1)} %get-tuple-element.14, f32[1024,256]{1,0:T(8,128)S(1)} %get-tuple-element.12, f32[1024,256]{1,0:T(8,128)S(1)} %get-tuple-element.7), kind=kOutput, calls=%fused_computation.65 | convolution fusion | flops 3224371200 | bytes 8388608 | tf_op jit(solution)/shard_map/dot_general | solution.py:11
  18.1 3.0 %collective-permute-start.1 = (f32[512,1024]{1,0:T(8,128)}, f32[512,1024]{1,0:T(8,128)}, u32[]{:S(2)}, u32[]{:S(2)}) collective-permute-start(f32[512,1024]{1,0:T(8,128)} %fusion.59), channel_id=1, source_target_pairs={{0,8},{4,12},{8,0},{12,4},{1,9},{5,13},{9,1},{13,5},{2,10},{6,14},... | collective-permute-start | bytes 6291464 | tf_op jit(solution)/shard_map/ppermute | solution.py:22
  21.5 2.0 fusion.98
  23.5 1.7 fusion.102
  25.2 1.1 pad_maximum_fusion.8
  26.8 6.1 %fusion.38 = f32[256,1024]{1,0:T(8,128)} fusion(f32[1024,256]{1,0:T(8,128)} %copy-done.19, f32[1024,256]{1,0:T(8,128)} %copy-done.21, f32[1024,256]{1,0:T(8,128)} %copy-done.22, f32[1024,256]{1,0:T(8,128)} %copy-done.20), kind=kOutput, calls=%fused_computation.41 | convolution fusion | flops 1613758464 | bytes 5242880 | tf_op jit(solution)/shard_map/dot_general | solution.py:15
  33.0 56.5 %collective-permute-done.7 = f32[256,1024]{1,0:T(8,128)} collective-permute-done((f32[256,1024]{1,0:T(8,128)}, f32[256,1024]{1,0:T(8,128)}, u32[]{:S(2)}, u32[]{:S(2)}) %collective-permute-start.7) | collective-permute-done | bytes 1048608 | tf_op jit(solution)/shard_map/ppermute | solution.py:22
  89.5 0.6 fusion.161
  94.3 0.6 collective-permute-start.2
  95.1 4.4 %constant_dynamic-slice_fusion.13 = (f32[512,512]{1,0:T(8,128)}, f32[512,512]{1,0:T(8,128)}, f32[512,512]{1,0:T(8,128)}, f32[512,512]{1,0:T(8,128)}) fusion(f32[512,2048]{1,0:T(8,128)} %param.10, s32[]{:T(128)S(6)} %select_n.52, s32[]{:T(128)S(6)} %select_n.53, s32[]{:T(128)S(6)} %select_n.55, s32[]{:T(128)S(6)} %select_n.54), kind=kLoop, calls=%fused_computation.151 | loop fusion | bytes 8388624 | tf_op jit(solution)/shard_map/dynamic_slice | solution.py:30
  99.6 2.0 fusion.92
  101.6 2.1 fusion.95
  103.7 4.5 %pad_maximum_fusion.2 = f32[1024,1024]{1,0:T(8,128)} fusion(f32[256,1024]{1,0:T(8,128)} %collective-permute-done.8, f32[256,1024]{1,0:T(8,128)} %collective-permute-done.7, f32[256,1024]{1,0:T(8,128)} %collective-permute-done.6, f32[256,512]{1,0:T(8,128)S(1)} %fusion.98, f32[256,512]{1,0:T(8,128)S(1)} %fusion.102), kind=kLoop, calls=%fused_computation.24 | loop fusion | flops 4194304 | bytes 8388608 | tf_op jit(solution)/shard_map/concatenate | solution.py:101
  108.2 62.1 %all-gather.7.cloned.1.call-done = f32[2048,1024]{1,0:T(8,128)} async-done(((f32[512,1024]{1,0:T(8,128)}), f32[2048,1024]{1,0:T(8,128)}) %all-gather.7.cloned.1.call-update) | async-done | bytes 8388624 | tf_op jit(solution)/shard_map/all_gather | solution.py:85
  170.3 5.0 %fusion.69 = f32[512,512]{1,0:T(8,128)} fusion(f32[512,512]{1,0:T(8,128)S(1)} %copy-done.8, f32[1024,1024]{1,0:T(8,128)} %pad_maximum_fusion.2, f32[4,512,1024]{2,1,0:T(8,128)} %bitcast.104, s32[]{:T(128)S(6)} %select_n.58), kind=kOutput, calls=%fused_computation.67 | convolution fusion | flops 1610874880 | bytes 6291460 | tf_op jit(solution)/shard_map/dot_general | solution.py:11
  175.3 1.5 collective-permute-start.16
  176.8 3.2 %fusion.156 = (f32[512,256]{1,0:T(8,128)}, f32[512,256]{1,0:T(8,128)}, f32[512,256]{1,0:T(8,128)}, f32[512,256]{1,0:T(8,128)}) fusion(f32[512,1024]{1,0:T(8,128)} %collective-permute-done), kind=kLoop, calls=%fused_computation.179 | loop fusion | bytes 4194304 | tf_op jit(solution)/shard_map/slice | solution.py:61
  180.0 3.2 %fusion.157 = (f32[512,512]{1,0:T(8,128)}, f32[512,512]{1,0:T(8,128)}) fusion(f32[512,1024]{1,0:T(8,128)} %collective-permute-done.1), kind=kLoop, calls=%fused_computation.180 | loop fusion | bytes 4194304 | tf_op jit(solution)/shard_map/slice | solution.py:61
  183.2 2.9 %fusion.158 = (f32[512,256]{1,0:T(8,128)}, f32[512,256]{1,0:T(8,128)}, f32[512,256]{1,0:T(8,128)}, f32[512,256]{1,0:T(8,128)}) fusion(f32[512,1024]{1,0:T(8,128)} %collective-permute-done.2), kind=kLoop, calls=%fused_computation.181 | loop fusion | bytes 4194304 | tf_op jit(solution)/shard_map/slice | solution.py:61
  186.1 4.6 %fusion.64 = f32[512,512]{1,0:T(8,128)} fusion(f32[512,512]{1,0:T(8,128)S(1)} %copy-done.6, f32[1024,1024]{1,0:T(8,128)S(1)} %copy-done.2, f32[4,512,1024]{2,1,0:T(8,128)} %bitcast.105, s32[]{:T(128)S(6)} %select_n.57), kind=kOutput, calls=%fused_computation.66 | convolution fusion | flops 1610874880 | bytes 6291460 | tf_op jit(solution)/shard_map/dot_general | solution.py:11
  190.7 0.7 collective-permute-start.10
  191.3 10.3 %collective-permute-done.16 = f32[512,512]{1,0:T(8,128)} collective-permute-done((f32[512,512]{1,0:T(8,128)}, f32[512,512]{1,0:T(8,128)}, u32[]{:S(2)}, u32[]{:S(2)}) %collective-permute-start.16) | collective-permute-done | bytes 1048608 | tf_op jit(solution)/shard_map/ppermute | solution.py:22
  201.7 18.3 %multiply_reduce_fusion.1 = f32[1024]{0:T(1024)S(1)} fusion(f32[512,1024]{1,0:T(8,128)} %fusion.59, f32[512,256]{1,0:T(8,128)} %get-tuple-element.26, f32[512,256]{1,0:T(8,128)} %get-tuple-element.27, f32[512,256]{1,0:T(8,128)} %get-tuple-element.28, f32[512,256]{1,0:T(8,128)} %get-tuple-element.25, f32[512,512]{1,0:T(8,128)} %get-tuple-element.24, ...), kind=kOutput, calls=%fused_computation.54 | convolution fusion | flops 6467615744 | bytes 12587008 | tf_op jit(solution)/shard_map/dot_general | solution.py:11
  220.0 0.6 collective-permute-start.9
  220.6 2.7 collective-permute-done.10
  223.3 6.7 %multiply_reduce_fusion.2 = (f32[512]{0:T(512)S(1)}, f32[512,512]{1,0:T(8,128)S(1)}) fusion(f32[512,512]{1,0:T(8,128)S(1)} %copy-done.8, f32[512,512]{1,0:T(8,128)} %collective-permute-done.17, f32[512,512]{1,0:T(8,128)} %collective-permute-done.16, f32[512,512]{1,0:T(8,128)} %collective-permute-done.15, f32[512,512]{1,0:T(8,128)} %fusion.69, ...), kind=kOutput, calls=%fused_computation.88 | convolution fusion | flops 3228302848 | bytes 10487808 | tf_op jit(solution)/shard_map/dot_general | solution.py:11
  230.0 3.8 %fusion.40 = f32[1024,512]{1,0:T(8,128)S(1)} fusion(f32[512,512]{1,0:T(8,128)S(1)} %get-tuple-element.48, f32[4,512,1024]{2,1,0:T(8,128)} %bitcast.106, s32[]{:T(128)S(6)} %select_n.58), kind=kOutput, calls=%fused_computation.44 | convolution fusion | flops 1610612736 | bytes 5242884 | tf_op jit(solution)/shard_map/dot_general | solution.py:15
  233.9 0.9 fusion.155
  235.3 5.1 %multiply_reduce_fusion.3 = (f32[512]{0:T(512)S(1)}, f32[512,512]{1,0:T(8,128)S(1)}) fusion(f32[512,512]{1,0:T(8,128)S(1)} %copy-done.7, f32[512,512]{1,0:T(8,128)S(1)} %collective-permute-done.11, f32[512,512]{1,0:T(8,128)} %collective-permute-done.10, f32[512,512]{1,0:T(8,128)S(1)} %collective-permute-done.9, f32[512,512]{1,0:T(8,128)} %fusion.64, ...), kind=kOutput, calls=%fused_computation.93 | convolution fusion | flops 3228302848 | bytes 10487808 | tf_op jit(solution)/shard_map/dot_general | solution.py:11
  240.4 3.8 %fusion.44 = f32[1024,512]{1,0:T(8,128)S(1)} fusion(f32[512,512]{1,0:T(8,128)S(1)} %get-tuple-element.52, f32[4,512,1024]{2,1,0:T(8,128)} %bitcast.107, s32[]{:T(128)S(6)} %select_n.57), kind=kOutput, calls=%fused_computation.48 | convolution fusion | flops 1610612736 | bytes 5242884 | tf_op jit(solution)/shard_map/dot_general | solution.py:15
  244.2 1.0 fusion.154
  246.2 0.9 slice_add_fusion
  247.1 1.5 collective-permute-start.20
  249.1 0.9 slice_add_fusion.2
  250.0 1.5 collective-permute-start.14
  251.4 10.7 %collective-permute-done.5 = f32[256]{0:T(256)S(1)} collective-permute-done((f32[256]{0:T(256)S(1)}, f32[256]{0:T(256)S(1)}, u32[]{:S(2)}, u32[]{:S(2)}) %collective-permute-start.5) | collective-permute-done | bytes 1056 | tf_op jit(solution)/shard_map/ppermute | solution.py:22
  262.2 0.6 add_add_fusion
  262.7 3.7 %multiply_reduce_fusion.5 = (f32[512]{0:T(512)S(1)}, f32[256,512]{1,0:T(8,128)S(1)}) fusion(f32[256,512]{1,0:T(8,128)S(1)} %fusion.98, f32[256,512]{1,0:T(8,128)} %collective-permute-done.20, f32[256,512]{1,0:T(8,128)} %collective-permute-done.18, f32[1024,512]{1,0:T(8,128)S(1)} %fusion.40, f32[1024,1024]{1,0:T(8,128)} %pad_maximum_fusion.2, ...), kind=kOutput, calls=%fused_computation.115 | convolution fusion | flops 806092288 | bytes 5769220 | tf_op jit(solution)/shard_map/dot_general | solution.py:11
  266.5 6.0 %collective-permute-done.14 = f32[256,512]{1,0:T(8,128)} collective-permute-done((f32[256,512]{1,0:T(8,128)}, f32[256,512]{1,0:T(8,128)}, u32[]{:S(2)}, u32[]{:S(2)}) %collective-permute-start.14) | collective-permute-done | bytes 524320 | tf_op jit(solution)/shard_map/ppermute | solution.py:22
  272.5 3.1 %multiply_reduce_fusion.6 = (f32[512]{0:T(512)S(1)}, f32[256,512]{1,0:T(8,128)S(1)}) fusion(f32[256,512]{1,0:T(8,128)S(1)} %fusion.102, f32[256,512]{1,0:T(8,128)} %collective-permute-done.14, f32[256,512]{1,0:T(8,128)} %collective-permute-done.12, f32[1024,512]{1,0:T(8,128)} %copy-done.5, f32[1024,1024]{1,0:T(8,128)S(1)} %copy-done.3, ...), kind=kOutput, calls=%fused_computation.118 | convolution fusion | flops 806092288 | bytes 5769220 | tf_op jit(solution)/shard_map/dot_general | solution.py:11
  275.8 1.5 pad_maximum_fusion.5
  277.8 1.5 collective-permute-start.23
  279.3 1.0 pad_maximum_fusion.9
  280.3 1.1 collective-permute-done.23
  281.4 0.6 fusion.140
  (115 shorter events, 5.3 us)
Async XLA Ops:
  7.2 5.8 %copy-start = (f32[1,512,1024]{2,1,0:T(8,128)S(1)}, f32[1,512,1024]{2,1,0:T(8,128)}, u32[]{:S(2)}) copy-start(f32[1,512,1024]{2,1,0:T(8,128)} %param.11) | copy-start | bytes 6291460
  7.2 163.1 %all-gather.7.cloned.1.call-start = ((), (), s32[]{:S(2)}) async-start(), calls=%async_computation.1 | async-start | bytes 10485760 | tf_op jit(solution)/shard_map/all_gather | solution.py:85
  8.8 9.0 %copy-start.19 = (f32[1024,256]{1,0:T(8,128)}, f32[1024,256]{1,0:T(8,128)S(1)}, u32[]{:S(2)}) copy-start(f32[1024,256]{1,0:T(8,128)S(1)} %get-tuple-element.7) | copy-start | bytes 3145732
  12.9 8.1 %copy-start.24 = (s32[2,4]{1,0:T(2,128)S(1)}, s32[2,4]{1,0:T(2,128)}, u32[]{:S(2)}) copy-start(s32[2,4]{1,0:T(2,128)} %param.18) | copy-start | bytes 100
  12.9 8.1 %copy-start.26 = (s32[2]{0:T(128)S(1)}, s32[2]{0:T(128)}, u32[]{:S(2)}) copy-start(s32[2]{0:T(128)} %param.17) | copy-start | bytes 28
  17.8 5.7 %copy-start.4 = (f32[2,512,512]{2,1,0:T(8,128)S(1)}, f32[2,512,512]{2,1,0:T(8,128)}, u32[]{:S(2)}) copy-start(f32[2,512,512]{2,1,0:T(8,128)} %param.15) | copy-start | bytes 6291460
  17.8 244.9 %all-gather.5.cloned.1.call-start = ((), (), s32[]{:S(2)}) async-start(), calls=%async_computation | async-start | bytes 5242880 | tf_op jit(solution)/shard_map/all_gather | solution.py:88
  18.1 76.3 %collective-permute-start.1 = (f32[512,1024]{1,0:T(8,128)}, f32[512,1024]{1,0:T(8,128)}, u32[]{:S(2)}, u32[]{:S(2)}) collective-permute-start(f32[512,1024]{1,0:T(8,128)} %fusion.59), channel_id=1, source_target_pairs={{0,8},{4,12},{8,0},{12,4},{1,9},{5,13},{9,1},{13,5},{2,10},{6,14},... | collective-permute-start | bytes 6291464 | tf_op jit(solution)/shard_map/ppermute | solution.py:22
  26.3 6.7 %copy-start.25 = (s32[2,8]{1,0:T(2,128)S(1)}, s32[2,8]{1,0:T(2,128)}, u32[]{:S(2)}) copy-start(s32[2,8]{1,0:T(2,128)} %param.19) | copy-start | bytes 196
  26.3 63.2 %copy-start.23 = (s32[2]{0:T(128)S(1)}, s32[2]{0:T(128)}, u32[]{:S(2)}) copy-start(s32[2]{0:T(128)} %param.16) | copy-start | bytes 28
  26.3 63.2 %collective-permute-start.7 = (f32[256,1024]{1,0:T(8,128)}, f32[256,1024]{1,0:T(8,128)}, u32[]{:S(2)}, u32[]{:S(2)}) collective-permute-start(f32[256,1024]{1,0:T(8,128)} %pad_maximum_fusion.8), channel_id=1, source_target_pairs={{0,8},{4,12},{8,0},{12,4},{1,9},{5,13},{9,1},{13,5},{2,10},{6,14},... | collective-permute-start | bytes 3145736 | tf_op jit(solution)/shard_map/ppermute | solution.py:22
  26.3 150.5 %collective-permute-start = (f32[512,1024]{1,0:T(8,128)}, f32[512,1024]{1,0:T(8,128)}, u32[]{:S(2)}, u32[]{:S(2)}) collective-permute-start(f32[512,1024]{1,0:T(8,128)} %fusion.59), channel_id=1, source_target_pairs={{0,4},{4,0},{8,12},{12,8},{1,5},{5,1},{9,13},{13,9},{2,6},{6,2},{1... | collective-permute-start | bytes 6291464 | tf_op jit(solution)/shard_map/ppermute | solution.py:22
  26.3 77.4 %collective-permute-start.6 = (f32[256,1024]{1,0:T(8,128)}, f32[256,1024]{1,0:T(8,128)}, u32[]{:S(2)}, u32[]{:S(2)}) collective-permute-start(f32[256,1024]{1,0:T(8,128)} %pad_maximum_fusion.8), channel_id=1, source_target_pairs={{0,4},{4,0},{8,12},{12,8},{1,5},{5,1},{9,13},{13,9},{2,6},{6,2},{1... | collective-permute-start | bytes 3145736 | tf_op jit(solution)/shard_map/ppermute | solution.py:22
  89.5 14.2 %collective-permute-start.8 = (f32[256,1024]{1,0:T(8,128)}, f32[256,1024]{1,0:T(8,128)}, u32[]{:S(2)}, u32[]{:S(2)}) collective-permute-start(f32[256,1024]{1,0:T(8,128)} %collective-permute-done.7), channel_id=1, source_target_pairs={{0,4},{4,0},{8,12},{12,8},{1,5},{5,1},{9,13},{13,9},{2,6},{6,2},{1... | collective-permute-start | bytes 3145736 | tf_op jit(solution)/shard_map/ppermute | solution.py:22
  94.3 88.9 %collective-permute-start.2 = (f32[512,1024]{1,0:T(8,128)}, f32[512,1024]{1,0:T(8,128)}, u32[]{:S(2)}, u32[]{:S(2)}) collective-permute-start(f32[512,1024]{1,0:T(8,128)} %collective-permute-done.1), channel_id=1, source_target_pairs={{0,4},{4,0},{8,12},{12,8},{1,5},{5,1},{9,13},{13,9},{2,6},{6,2},{1... | collective-permute-start | bytes 6291464 | tf_op jit(solution)/shard_map/ppermute | solution.py:22
  103.7 66.6 %copy-start.8 = (f32[512,512]{1,0:T(8,128)S(1)}, f32[512,512]{1,0:T(8,128)}, u32[]{:S(2)}) copy-start(f32[512,512]{1,0:T(8,128)} %fusion.92) | copy-start | bytes 3145732
  175.3 26.3 %collective-permute-start.16 = (f32[512,512]{1,0:T(8,128)}, f32[512,512]{1,0:T(8,128)}, u32[]{:S(2)}, u32[]{:S(2)}) collective-permute-start(f32[512,512]{1,0:T(8,128)} %fusion.69), channel_id=1, source_target_pairs={{0,8},{4,12},{8,0},{12,4},{1,9},{5,13},{9,1},{13,5},{2,10},{6,14},... | collective-permute-start | bytes 3145736 | tf_op jit(solution)/shard_map/ppermute | solution.py:22
  180.0 6.1 %copy-start.2 = (f32[1024,1024]{1,0:T(8,128)S(1)}, f32[1024,1024]{1,0:T(8,128)}, u32[]{:S(2)}) copy-start(f32[1024,1024]{1,0:T(8,128)} %pad_maximum_fusion.2) | copy-start | bytes 12582916
  180.0 6.1 %copy-start.6 = (f32[512,512]{1,0:T(8,128)S(1)}, f32[512,512]{1,0:T(8,128)}, u32[]{:S(2)}) copy-start(f32[512,512]{1,0:T(8,128)} %fusion.95) | copy-start | bytes 3145732
  186.1 37.1 %collective-permute-start.15 = (f32[512,512]{1,0:T(8,128)}, f32[512,512]{1,0:T(8,128)}, u32[]{:S(2)}, u32[]{:S(2)}) collective-permute-start(f32[512,512]{1,0:T(8,128)} %fusion.69), channel_id=1, source_target_pairs={{0,4},{4,0},{8,12},{12,8},{1,5},{5,1},{9,13},{13,9},{2,6},{6,2},{1... | collective-permute-start | bytes 3145736 | tf_op jit(solution)/shard_map/ppermute | solution.py:22
  190.7 32.6 %collective-permute-start.10 = (f32[512,512]{1,0:T(8,128)}, f32[512,512]{1,0:T(8,128)}, u32[]{:S(2)}, u32[]{:S(2)}) collective-permute-start(f32[512,512]{1,0:T(8,128)} %fusion.64), channel_id=1, source_target_pairs={{0,8},{4,12},{8,0},{12,4},{1,9},{5,13},{9,1},{13,5},{2,10},{6,14},... | collective-permute-start | bytes 3145736 | tf_op jit(solution)/shard_map/ppermute | solution.py:22
  201.7 21.6 %collective-permute-start.17 = (f32[512,512]{1,0:T(8,128)}, f32[512,512]{1,0:T(8,128)}, u32[]{:S(2)}, u32[]{:S(2)}) collective-permute-start(f32[512,512]{1,0:T(8,128)} %collective-permute-done.16), channel_id=1, source_target_pairs={{0,4},{4,0},{8,12},{12,8},{1,5},{5,1},{9,13},{13,9},{2,6},{6,2},{1... | collective-permute-start | bytes 3145736 | tf_op jit(solution)/shard_map/ppermute | solution.py:22
  201.7 21.6 %copy-start.14 = (f32[512,512]{1,0:T(8,128)S(1)}, f32[512,512]{1,0:T(8,128)}, u32[]{:S(2)}) copy-start(f32[512,512]{1,0:T(8,128)} %get-tuple-element.8) | copy-start | bytes 3145732
  220.0 15.2 %collective-permute-start.9 = (f32[512,512]{1,0:T(8,128)}, f32[512,512]{1,0:T(8,128)S(1)}, u32[]{:S(2)}, u32[]{:S(2)}) collective-permute-start(f32[512,512]{1,0:T(8,128)} %fusion.64), channel_id=1, source_target_pairs={{0,4},{4,0},{8,12},{12,8},{1,5},{5,1},{9,13},{13,9},{2,6},{6,2},{1... | collective-permute-start | bytes 3145736 | tf_op jit(solution)/shard_map/ppermute | solution.py:22
  223.3 12.0 %collective-permute-start.11 = (f32[512,512]{1,0:T(8,128)}, f32[512,512]{1,0:T(8,128)S(1)}, u32[]{:S(2)}, u32[]{:S(2)}) collective-permute-start(f32[512,512]{1,0:T(8,128)} %collective-permute-done.10), channel_id=1, source_target_pairs={{0,4},{4,0},{8,12},{12,8},{1,5},{5,1},{9,13},{13,9},{2,6},{6,2},{1... | collective-permute-start | bytes 3145736 | tf_op jit(solution)/shard_map/ppermute | solution.py:22
  230.0 10.4 %copy-start.9 = (f32[512,512]{1,0:T(8,128)}, f32[512,512]{1,0:T(8,128)S(1)}, u32[]{:S(2)}) copy-start(f32[512,512]{1,0:T(8,128)S(1)} %get-tuple-element.48) | copy-start | bytes 3145732
  230.0 5.2 %copy-start.7 = (f32[512,512]{1,0:T(8,128)S(1)}, f32[512,512]{1,0:T(8,128)}, u32[]{:S(2)}) copy-start(f32[512,512]{1,0:T(8,128)} %fusion.95) | copy-start | bytes 3145732
  230.0 5.2 %copy-start.15 = (f32[512,512]{1,0:T(8,128)S(1)}, f32[512,512]{1,0:T(8,128)}, u32[]{:S(2)}) copy-start(f32[512,512]{1,0:T(8,128)} %get-tuple-element.8) | copy-start | bytes 3145732
  230.0 5.2 %copy-start.16 = (f32[512,512]{1,0:T(8,128)S(1)}, f32[512,512]{1,0:T(8,128)}, u32[]{:S(2)}) copy-start(f32[512,512]{1,0:T(8,128)} %get-tuple-element.9) | copy-start | bytes 3145732
  230.0 5.2 %copy-start.17 = (f32[512,512]{1,0:T(8,128)S(1)}, f32[512,512]{1,0:T(8,128)}, u32[]{:S(2)}) copy-start(f32[512,512]{1,0:T(8,128)} %get-tuple-element.10) | copy-start | bytes 3145732
  230.0 5.2 %copy-start.18 = (f32[512,512]{1,0:T(8,128)S(1)}, f32[512,512]{1,0:T(8,128)}, u32[]{:S(2)}) copy-start(f32[512,512]{1,0:T(8,128)} %get-tuple-element.11) | copy-start | bytes 3145732
  234.7 11.4 %collective-permute-start.19 = (f32[256,512]{1,0:T(8,128)S(1)}, f32[256,512]{1,0:T(8,128)S(1)}, u32[]{:S(2)}, u32[]{:S(2)}) collective-permute-start(f32[256,512]{1,0:T(8,128)S(1)} %get-tuple-element.18), channel_id=1, source_target_pairs={{0,4},{4,0},{8,12},{12,8},{1,5},{5,1},{9,13},{13,9},{2,6},{6,2},{1... | collective-permute-start | bytes 1572872 | tf_op jit(solution)/shard_map/ppermute | solution.py:22
  240.4 6.7 %copy-start.11 = (f32[512,512]{1,0:T(8,128)}, f32[512,512]{1,0:T(8,128)S(1)}, u32[]{:S(2)}) copy-start(f32[512,512]{1,0:T(8,128)S(1)} %get-tuple-element.52) | copy-start | bytes 3145732
  245.1 3.9 %collective-permute-start.13 = (f32[256,512]{1,0:T(8,128)S(1)}, f32[256,512]{1,0:T(8,128)S(1)}, u32[]{:S(2)}, u32[]{:S(2)}) collective-permute-start(f32[256,512]{1,0:T(8,128)S(1)} %get-tuple-element.16), channel_id=1, source_target_pairs={{0,4},{4,0},{8,12},{12,8},{1,5},{5,1},{9,13},{13,9},{2,6},{6,2},{1... | collective-permute-start | bytes 1572872 | tf_op jit(solution)/shard_map/ppermute | solution.py:22
  245.2 3.3 %collective-permute-start.4 = (f32[256]{0:T(256)S(1)}, f32[256]{0:T(256)S(1)}, u32[]{:S(2)}, u32[]{:S(2)}) collective-permute-start(f32[256]{0:T(256)S(1)} %get-tuple-element.38), channel_id=1, source_target_pairs={{0,4},{4,0},{8,12},{12,8},{1,5},{5,1},{9,13},{13,9},{2,6},{6,2},{1... | collective-permute-start | bytes 3080 | tf_op jit(solution)/shard_map/ppermute | solution.py:22
  245.7 4.3 %collective-permute-start.3 = (f32[256]{0:T(256)S(1)}, f32[256]{0:T(256)S(1)}, u32[]{:S(2)}, u32[]{:S(2)}) collective-permute-start(f32[256]{0:T(256)S(1)} %get-tuple-element.37), channel_id=1, source_target_pairs={{0,4},{4,0},{8,12},{12,8},{1,5},{5,1},{9,13},{13,9},{2,6},{6,2},{1... | collective-permute-start | bytes 3080 | tf_op jit(solution)/shard_map/ppermute | solution.py:22
  245.7 17.0 %collective-permute-start.18 = (f32[256,512]{1,0:T(8,128)}, f32[256,512]{1,0:T(8,128)}, u32[]{:S(2)}, u32[]{:S(2)}) collective-permute-start(f32[256,512]{1,0:T(8,128)} %get-tuple-element.17), channel_id=1, source_target_pairs={{0,4},{4,0},{8,12},{12,8},{1,5},{5,1},{9,13},{13,9},{2,6},{6,2},{1... | collective-permute-start | bytes 1572872 | tf_op jit(solution)/shard_map/ppermute | solution.py:22
  247.1 15.7 %collective-permute-start.20 = (f32[256,512]{1,0:T(8,128)}, f32[256,512]{1,0:T(8,128)}, u32[]{:S(2)}, u32[]{:S(2)}) collective-permute-start(f32[256,512]{1,0:T(8,128)} %slice_add_fusion), channel_id=1, source_target_pairs={{0,8},{4,12},{8,0},{12,4},{1,9},{5,13},{9,1},{13,5},{2,10},{6,14},... | collective-permute-start | bytes 1572872 | tf_op jit(solution)/shard_map/ppermute | solution.py:22
  248.5 13.6 %collective-permute-start.5 = (f32[256]{0:T(256)S(1)}, f32[256]{0:T(256)S(1)}, u32[]{:S(2)}, u32[]{:S(2)}) collective-permute-start(f32[256]{0:T(256)S(1)} %slice_add_fusion.4), channel_id=1, source_target_pairs={{0,8},{4,12},{8,0},{12,4},{1,9},{5,13},{9,1},{13,5},{2,10},{6,14},... | collective-permute-start | bytes 3080 | tf_op jit(solution)/shard_map/ppermute | solution.py:22
  249.1 17.4 %collective-permute-start.12 = (f32[256,512]{1,0:T(8,128)}, f32[256,512]{1,0:T(8,128)}, u32[]{:S(2)}, u32[]{:S(2)}) collective-permute-start(f32[256,512]{1,0:T(8,128)} %get-tuple-element.15), channel_id=1, source_target_pairs={{0,4},{4,0},{8,12},{12,8},{1,5},{5,1},{9,13},{13,9},{2,6},{6,2},{1... | collective-permute-start | bytes 1572872 | tf_op jit(solution)/shard_map/ppermute | solution.py:22
  250.0 22.5 %collective-permute-start.14 = (f32[256,512]{1,0:T(8,128)}, f32[256,512]{1,0:T(8,128)}, u32[]{:S(2)}, u32[]{:S(2)}) collective-permute-start(f32[256,512]{1,0:T(8,128)} %slice_add_fusion.2), channel_id=1, source_target_pairs={{0,8},{4,12},{8,0},{12,4},{1,9},{5,13},{9,1},{13,5},{2,10},{6,14},... | collective-permute-start | bytes 1572872 | tf_op jit(solution)/shard_map/ppermute | solution.py:22
  262.7 9.8 %copy-start.3 = (f32[1024,1024]{1,0:T(8,128)S(1)}, f32[1024,1024]{1,0:T(8,128)}, u32[]{:S(2)}) copy-start(f32[1024,1024]{1,0:T(8,128)} %pad_maximum_fusion.2) | copy-start | bytes 12582916
  266.5 9.3 %copy-start.10 = (f32[512,512]{1,0:T(8,128)S(1)}, f32[512,512]{1,0:T(8,128)}, u32[]{:S(2)}) copy-start(f32[512,512]{1,0:T(8,128)} %copy-done.9) | copy-start | bytes 3145732
  266.5 9.3 %copy-start.12 = (f32[512,512]{1,0:T(8,128)S(1)}, f32[512,512]{1,0:T(8,128)}, u32[]{:S(2)}) copy-start(f32[512,512]{1,0:T(8,128)} %copy-done.11) | copy-start | bytes 3145732
  272.5 9.4 %copy-start.1 = (f32[1,512,1024]{2,1,0:T(8,128)S(1)}, f32[1,512,1024]{2,1,0:T(8,128)}, u32[]{:S(2)}) copy-start(f32[1,512,1024]{2,1,0:T(8,128)} %param.11) | copy-start | bytes 6291460
  275.7 2.1 collective-permute-start.22
  277.3 3.0 %collective-permute-start.21 = (f32[2,128]{1,0:T(2,128)S(1)}, f32[2,128]{1,0:T(2,128)S(1)}, u32[]{:S(2)}, u32[]{:S(2)}) collective-permute-start(f32[2,128]{1,0:T(2,128)S(1)} %get-tuple-element.29), channel_id=1, source_target_pairs={{0,4},{4,0},{8,12},{12,8},{1,5},{5,1},{9,13},{13,9},{2,6},{6,2},{1... | collective-permute-start | bytes 3080 | tf_op jit(solution)/shard_map/ppermute | solution.py:22
  277.8 3.6 %collective-permute-start.23 = (f32[2,128]{1,0:T(2,128)S(1)}, f32[2,128]{1,0:T(2,128)S(1)}, u32[]{:S(2)}, u32[]{:S(2)}) collective-permute-start(f32[2,128]{1,0:T(2,128)S(1)} %fusion.146), channel_id=1, source_target_pairs={{0,8},{4,12},{8,0},{12,4},{1,9},{5,13},{9,1},{13,5},{2,10},{6,14},... | collective-permute-start | bytes 3080 | tf_op jit(solution)/shard_map/ppermute | solution.py:22
  (5 other events, 13.3 us)
Sparse Core Ops, SparseCore 0:
  17.9 152.3 all-gather.6
  171.9 78.9 all-gather.4

commit v2 on v1

--- a/solution.py
+++ b/solution.py
@@ -109,6 +109,8 @@
     own_squares = jnp.sum(inverse[:, :node_rows] ** 2, axis=0)
     var_one = (own_squares + row_sum([terms[d] for d in range(n)]))[None, :]
 
+    all_factors, var_one = lax.optimization_barrier((all_factors, var_one))
+
     parent_factor = [
         lax.dynamic_index_in_dim(all_factors, parents[i], 0, False) for i in range(nodes)
     ]

time: 289 us -> 284 us (0.983)
  matrix products: 72.9 us -> 65.5 us
    all_gather x1, waiting for transfers between devices: 62.1 us -> 38.7 us  [body(): all_factors = lax.all_gather(factor, 'col', axis=0)]
    ppermute x24, waiting for transfers between devices: 87.3 us -> 105 us  [swap(): return lax.ppermute(block, 'row', [(i, i ^ bit) for i in range(n)])]
    all_gather x1, waiting for transfers between devices: 0.01 us -> 4.88 us  [body(): all_grams = lax.all_gather(gram, 'col', axis=0)]
    dot_general x3, matrix products: 13.8 us -> 9.15 us  [crossed(): lax.dot_general(left, right, (((0,), (0,)), ((), ())), precision=PRECISIO...]
  transfers between devices with their start and end apart: 26 -> 26, of which waited for: 7 -> 9; matrix products, arithmetic and copies ran while one was open for 32% -> 30% of each run, Pallas kernels for 0% -> 0%
where the time goes in v2:
time: 284 us; the launch traced here: 283 us
  waiting for transfers between devices  149 us (52%)
  matrix products  65.5 us (23%)
  local copies, waits for them, and re-layouts  20.7 us (7%)
  between operations  18.4 us (6%)
  starting transfers between devices  15.6 us (5%)
  other arithmetic  14 us (5%)
    ppermute x24, waiting for transfers between devices, swap(): return lax.ppermute(block, 'row', [(i, i ^ bit) for i in range(n)])  105 us
    dot_general x12, matrix products, product(): jnp.dot(left, right, precision=PRECISION, preferred_element_type=jnp.floa...  56.4 us
    all_gather x1, waiting for transfers between devices, body(): all_factors = lax.all_gather(factor, 'col', axis=0)  38.7 us
    ppermute x24, starting transfers between devices, swap(): return lax.ppermute(block, 'row', [(i, i ^ bit) for i in range(n)])  15.4 us
    dot_general x3, matrix products, crossed(): lax.dot_general(left, right, (((0,), (0,)), ((), ())), precision=PRECISIO...  9.15 us
    slice x3, local copies, waits for them, and re-layouts, reordered(): block[:, (d ^ e) * share:((d ^ e) + 1) * share]  8.82 us
    dynamic_slice x2, local copies, waits for them, and re-layouts, own_first(): lax.dynamic_slice_in_dim(array, (me ^ d) * share, share, axis)  6.9 us
  transfers between devices with their start and end apart: 26, of which 9 were waited for; matrix products, arithmetic and copies ran while one was open for 30% of the time, Pallas kernels for 0%

profile of v2, /device:TPU:0, one launch (start us, length us, event | category | flops | bytes accessed | tf_op | source)
XLA Modules:
  0.0 283.1 jit_solution(10372713962109828890)
XLA Ops:
  7.3 1.5 multiply_reduce_fusion.4
  8.8 2.5 dynamic-slice_bitcast_fusion.2
  11.3 0.9 copy-done.17
  12.9 4.8 %fusion.59 = f32[512,1024]{1,0:T(8,128)} fusion(f32[1,512,1024]{2,1,0:T(8,128)S(1)} %copy-done, f32[1024,256]{1,0:T(8,128)S(1)} %get-tuple-element.17, f32[1024,256]{1,0:T(8,128)S(1)} %get-tuple-element.18, f32[1024,256]{1,0:T(8,128)S(1)} %get-tuple-element.16, f32[1024,256]{1,0:T(8,128)S(1)} %get-tuple-element.11), kind=kOutput, calls=%fused_computation.65 | convolution fusion | flops 3224371200 | bytes 8388608 | tf_op jit(solution)/shard_map/dot_general | solution.py:11
  18.0 3.0 %collective-permute-start.1 = (f32[512,1024]{1,0:T(8,128)}, f32[512,1024]{1,0:T(8,128)}, u32[]{:S(2)}, u32[]{:S(2)}) collective-permute-start(f32[512,1024]{1,0:T(8,128)} %fusion.59), channel_id=1, source_target_pairs={{0,8},{4,12},{8,0},{12,4},{1,9},{5,13},{9,1},{13,5},{2,10},{6,14},... | collective-permute-start | bytes 6291464 | tf_op jit(solution)/shard_map/ppermute | solution.py:22
  21.5 2.0 fusion.98
  23.5 43.5 %collective-permute-done.1 = f32[512,1024]{1,0:T(8,128)} collective-permute-done((f32[512,1024]{1,0:T(8,128)}, f32[512,1024]{1,0:T(8,128)}, u32[]{:S(2)}, u32[]{:S(2)}) %collective-permute-start.1) | collective-permute-done | bytes 2097184 | tf_op jit(solution)/shard_map/ppermute | solution.py:22
  67.0 1.7 fusion.102
  68.7 1.1 pad_maximum_fusion.8
  69.7 1.7 collective-permute-start.7
  71.7 5.4 %fusion.38 = f32[256,1024]{1,0:T(8,128)} fusion(f32[1024,256]{1,0:T(8,128)} %copy-done.16, f32[1024,256]{1,0:T(8,128)} %copy-done.18, f32[1024,256]{1,0:T(8,128)} %copy-done.19, f32[1024,256]{1,0:T(8,128)} %copy-done.17), kind=kOutput, calls=%fused_computation.41 | convolution fusion | flops 1613758464 | bytes 5242880 | tf_op jit(solution)/shard_map/dot_general | solution.py:15
  77.4 4.4 %constant_dynamic-slice_fusion.13 = (f32[512,512]{1,0:T(8,128)}, f32[512,512]{1,0:T(8,128)}, f32[512,512]{1,0:T(8,128)}, f32[512,512]{1,0:T(8,128)}) fusion(f32[512,2048]{1,0:T(8,128)} %param.10, s32[]{:T(128)S(6)} %select_n.52, s32[]{:T(128)S(6)} %select_n.53, s32[]{:T(128)S(6)} %select_n.55, s32[]{:T(128)S(6)} %select_n.54), kind=kLoop, calls=%fused_computation.151 | loop fusion | bytes 8388624 | tf_op jit(solution)/shard_map/dynamic_slice | solution.py:30
  81.8 2.0 fusion.92
  83.9 11.8 %collective-permute-done.7 = f32[256,1024]{1,0:T(8,128)} collective-permute-done((f32[256,1024]{1,0:T(8,128)}, f32[256,1024]{1,0:T(8,128)}, u32[]{:S(2)}, u32[]{:S(2)}) %collective-permute-start.7) | collective-permute-done | bytes 1048608 | tf_op jit(solution)/shard_map/ppermute | solution.py:22
  95.6 2.9 %fusion.156 = (f32[512,256]{1,0:T(8,128)}, f32[512,256]{1,0:T(8,128)}, f32[512,256]{1,0:T(8,128)}, f32[512,256]{1,0:T(8,128)}) fusion(f32[512,1024]{1,0:T(8,128)} %collective-permute-done), kind=kLoop, calls=%fused_computation.179 | loop fusion | bytes 4194304 | tf_op jit(solution)/shard_map/slice | solution.py:61
  98.5 3.1 %fusion.157 = (f32[512,512]{1,0:T(8,128)}, f32[512,512]{1,0:T(8,128)}) fusion(f32[512,1024]{1,0:T(8,128)} %collective-permute-done.1), kind=kLoop, calls=%fused_computation.180 | loop fusion | bytes 4194304 | tf_op jit(solution)/shard_map/slice | solution.py:61
  101.6 2.9 %fusion.158 = (f32[512,256]{1,0:T(8,128)}, f32[512,256]{1,0:T(8,128)}, f32[512,256]{1,0:T(8,128)}, f32[512,256]{1,0:T(8,128)}) fusion(f32[512,1024]{1,0:T(8,128)} %collective-permute-done.2), kind=kLoop, calls=%fused_computation.181 | loop fusion | bytes 4194304 | tf_op jit(solution)/shard_map/slice | solution.py:61
  104.5 17.1 %multiply_reduce_fusion.1 = f32[1024]{0:T(1024)S(1)} fusion(f32[512,1024]{1,0:T(8,128)} %fusion.59, f32[512,256]{1,0:T(8,128)} %get-tuple-element.30, f32[512,256]{1,0:T(8,128)} %get-tuple-element.31, f32[512,256]{1,0:T(8,128)} %get-tuple-element.32, f32[512,256]{1,0:T(8,128)} %get-tuple-element.29, f32[512,512]{1,0:T(8,128)} %get-tuple-element.28, ...), kind=kOutput, calls=%fused_computation.54 | convolution fusion | flops 6467615744 | bytes 12587008 | tf_op jit(solution)/shard_map/dot_general | solution.py:11
  122.2 0.6 fusion.161
  124.8 1.8 collective-permute-start.5
  126.6 4.4 %pad_maximum_fusion.2 = f32[1024,1024]{1,0:T(8,128)} fusion(f32[256,1024]{1,0:T(8,128)} %collective-permute-done.8, f32[256,1024]{1,0:T(8,128)} %collective-permute-done.7, f32[256,1024]{1,0:T(8,128)} %collective-permute-done.6, f32[256,512]{1,0:T(8,128)S(1)} %fusion.98, f32[256,512]{1,0:T(8,128)S(1)} %fusion.102), kind=kLoop, calls=%fused_computation.24 | loop fusion | flops 4194304 | bytes 8388608 | tf_op jit(solution)/shard_map/concatenate | solution.py:101
  131.6 38.7 %all-gather.5.cloned.1.call-done = f32[2048,1024]{1,0:T(8,128)} async-done(((f32[512,1024]{1,0:T(8,128)}), f32[2048,1024]{1,0:T(8,128)}) %all-gather.5.cloned.1.call-update) | async-done | bytes 8388624 | tf_op jit(solution)/shard_map/all_gather | solution.py:85
  170.3 5.3 %fusion.69 = f32[512,512]{1,0:T(8,128)} fusion(f32[512,512]{1,0:T(8,128)} %fusion.92, f32[1024,1024]{1,0:T(8,128)} %pad_maximum_fusion.2, f32[4,512,1024]{2,1,0:T(8,128)} %bitcast.104, s32[]{:T(128)S(6)} %select_n.58), kind=kOutput, calls=%fused_computation.67 | convolution fusion | flops 1610874880 | bytes 6291460 | tf_op jit(solution)/shard_map/dot_general | solution.py:11
  175.6 1.5 collective-permute-start.16
  179.2 2.5 fusion.95
  181.7 4.2 %fusion.64 = f32[512,512]{1,0:T(8,128)S(1)} fusion(f32[512,512]{1,0:T(8,128)S(1)} %fusion.95, f32[1024,1024]{1,0:T(8,128)} %pad_maximum_fusion.2, f32[4,512,1024]{2,1,0:T(8,128)} %bitcast.105, s32[]{:T(128)S(6)} %select_n.57), kind=kOutput, calls=%fused_computation.66 | convolution fusion | flops 1610874880 | bytes 6291460 | tf_op jit(solution)/shard_map/dot_general | solution.py:11
  186.0 0.6 collective-permute-start.10
  186.6 15.3 %collective-permute-done.16 = f32[512,512]{1,0:T(8,128)} collective-permute-done((f32[512,512]{1,0:T(8,128)}, f32[512,512]{1,0:T(8,128)}, u32[]{:S(2)}, u32[]{:S(2)}) %collective-permute-start.16) | collective-permute-done | bytes 1048608 | tf_op jit(solution)/shard_map/ppermute | solution.py:22
  202.4 21.0 %collective-permute-done.10 = f32[512,512]{1,0:T(8,128)S(1)} collective-permute-done((f32[512,512]{1,0:T(8,128)S(1)}, f32[512,512]{1,0:T(8,128)S(1)}, u32[]{:S(2)}, u32[]{:S(2)}) %collective-permute-start.10) | collective-permute-done | bytes 1048608 | tf_op jit(solution)/shard_map/ppermute | solution.py:22
  223.4 5.1 %multiply_reduce_fusion.2 = (f32[512]{0:T(512)S(1)}, f32[512,512]{1,0:T(8,128)S(1)}) fusion(f32[512,512]{1,0:T(8,128)S(1)} %copy-done.6, f32[512,512]{1,0:T(8,128)S(1)} %collective-permute-done.17, f32[512,512]{1,0:T(8,128)} %collective-permute-done.16, f32[512,512]{1,0:T(8,128)S(1)} %collective-permute-done.15, f32[512,512]{1,0:T(8,128)} %fusion.69, ...), kind=kOutput, calls=%fused_computation.88 | convolution fusion | flops 3228302848 | bytes 10487808 | tf_op jit(solution)/shard_map/dot_general | solution.py:11
  228.6 1.8 fusion.40
  230.4 1.0 fusion.155
  231.9 5.1 %multiply_reduce_fusion.3 = (f32[512]{0:T(512)S(1)}, f32[512,512]{1,0:T(8,128)S(1)}) fusion(f32[512,512]{1,0:T(8,128)S(1)} %fusion.95, f32[512,512]{1,0:T(8,128)} %collective-permute-done.11, f32[512,512]{1,0:T(8,128)S(1)} %collective-permute-done.10, f32[512,512]{1,0:T(8,128)S(1)} %collective-permute-done.9, f32[512,512]{1,0:T(8,128)S(1)} %fusion.64, ...), kind=kOutput, calls=%fused_computation.93 | convolution fusion | flops 3228302848 | bytes 10487808 | tf_op jit(solution)/shard_map/dot_general | solution.py:11
  237.0 1.8 fusion.44
  238.9 1.1 fusion.154
  240.5 0.9 slice_add_fusion
  241.4 1.5 collective-permute-start.20
  242.9 2.1 slice_add_fusion.2
  244.9 0.8 collective-permute-start.14
  246.0 4.9 %all-gather.7.cloned.1.call-done = f32[1024,1024]{1,0:T(8,128)} async-done(((f32[256,1024]{1,0:T(8,128)}), f32[1024,1024]{1,0:T(8,128)}) %all-gather.7.cloned.1.call-update) | async-done | bytes 4194320 | tf_op jit(solution)/shard_map/all_gather | solution.py:88
  250.9 5.6 %collective-permute-done.20 = f32[256,512]{1,0:T(8,128)} collective-permute-done((f32[256,512]{1,0:T(8,128)}, f32[256,512]{1,0:T(8,128)}, u32[]{:S(2)}, u32[]{:S(2)}) %collective-permute-start.20) | collective-permute-done | bytes 524320 | tf_op jit(solution)/shard_map/ppermute | solution.py:22
  256.5 3.4 %multiply_reduce_fusion.5 = (f32[512]{0:T(512)S(1)}, f32[256,512]{1,0:T(8,128)S(1)}) fusion(f32[256,512]{1,0:T(8,128)S(1)} %fusion.98, f32[256,512]{1,0:T(8,128)} %collective-permute-done.20, f32[256,512]{1,0:T(8,128)} %collective-permute-done.18, f32[1024,512]{1,0:T(8,128)} %copy-done.4, f32[1024,1024]{1,0:T(8,128)} %pad_maximum_fusion.2, ...), kind=kOutput, calls=%fused_computation.115 | convolution fusion | flops 806092288 | bytes 5769220 | tf_op jit(solution)/shard_map/dot_general | solution.py:11
  260.0 6.8 %collective-permute-done.14 = f32[256,512]{1,0:T(8,128)} collective-permute-done((f32[256,512]{1,0:T(8,128)}, f32[256,512]{1,0:T(8,128)}, u32[]{:S(2)}, u32[]{:S(2)}) %collective-permute-start.14) | collective-permute-done | bytes 524320 | tf_op jit(solution)/shard_map/ppermute | solution.py:22
  266.8 3.1 %multiply_reduce_fusion.6 = (f32[512]{0:T(512)S(1)}, f32[256,512]{1,0:T(8,128)S(1)}) fusion(f32[256,512]{1,0:T(8,128)S(1)} %fusion.102, f32[256,512]{1,0:T(8,128)} %collective-permute-done.14, f32[256,512]{1,0:T(8,128)} %collective-permute-done.12, f32[1024,512]{1,0:T(8,128)} %copy-done.5, f32[1024,1024]{1,0:T(8,128)S(1)} %copy-done.2, ...), kind=kOutput, calls=%fused_computation.118 | convolution fusion | flops 806092288 | bytes 5769220 | tf_op jit(solution)/shard_map/dot_general | solution.py:11
  270.1 1.5 pad_maximum_fusion.5
  272.1 1.5 collective-permute-start.23
  273.5 1.0 pad_maximum_fusion.9
  274.6 1.1 collective-permute-done.23
  (114 shorter events, 6.3 us)
Async XLA Ops:
  7.2 5.8 %copy-start = (f32[1,512,1024]{2,1,0:T(8,128)S(1)}, f32[1,512,1024]{2,1,0:T(8,128)}, u32[]{:S(2)}) copy-start(f32[1,512,1024]{2,1,0:T(8,128)} %param.11) | copy-start | bytes 6291460
  7.2 163.1 %all-gather.5.cloned.1.call-start = ((), (), s32[]{:S(2)}) async-start(), calls=%async_computation | async-start | bytes 10485760 | tf_op jit(solution)/shard_map/all_gather | solution.py:85
  12.9 8.1 %copy-start.21 = (s32[2,4]{1,0:T(2,128)S(1)}, s32[2,4]{1,0:T(2,128)}, u32[]{:S(2)}) copy-start(s32[2,4]{1,0:T(2,128)} %param.18) | copy-start | bytes 100
  12.9 8.1 %copy-start.23 = (s32[2]{0:T(128)S(1)}, s32[2]{0:T(128)}, u32[]{:S(2)}) copy-start(s32[2]{0:T(128)} %param.17) | copy-start | bytes 28
  17.8 49.2 %copy-start.3 = (f32[2,512,512]{2,1,0:T(8,128)S(1)}, f32[2,512,512]{2,1,0:T(8,128)}, u32[]{:S(2)}) copy-start(f32[2,512,512]{2,1,0:T(8,128)} %param.15) | copy-start | bytes 6291460
  17.8 233.1 %all-gather.7.cloned.1.call-start = ((), (), s32[]{:S(2)}) async-start(), calls=%async_computation.1 | async-start | bytes 5242880 | tf_op jit(solution)/shard_map/all_gather | solution.py:88
  18.0 49.0 %collective-permute-start.1 = (f32[512,1024]{1,0:T(8,128)}, f32[512,1024]{1,0:T(8,128)}, u32[]{:S(2)}, u32[]{:S(2)}) collective-permute-start(f32[512,1024]{1,0:T(8,128)} %fusion.59), channel_id=1, source_target_pairs={{0,8},{4,12},{8,0},{12,4},{1,9},{5,13},{9,1},{13,5},{2,10},{6,14},... | collective-permute-start | bytes 6291464 | tf_op jit(solution)/shard_map/ppermute | solution.py:22
  21.0 74.6 %collective-permute-start = (f32[512,1024]{1,0:T(8,128)}, f32[512,1024]{1,0:T(8,128)}, u32[]{:S(2)}, u32[]{:S(2)}) collective-permute-start(f32[512,1024]{1,0:T(8,128)} %fusion.59), channel_id=1, source_target_pairs={{0,4},{4,0},{8,12},{12,8},{1,5},{5,1},{9,13},{13,9},{2,6},{6,2},{1... | collective-permute-start | bytes 6291464 | tf_op jit(solution)/shard_map/ppermute | solution.py:22
  67.0 34.6 %collective-permute-start.2 = (f32[512,1024]{1,0:T(8,128)}, f32[512,1024]{1,0:T(8,128)}, u32[]{:S(2)}, u32[]{:S(2)}) collective-permute-start(f32[512,1024]{1,0:T(8,128)} %collective-permute-done.1), channel_id=1, source_target_pairs={{0,4},{4,0},{8,12},{12,8},{1,5},{5,1},{9,13},{13,9},{2,6},{6,2},{1... | collective-permute-start | bytes 6291464 | tf_op jit(solution)/shard_map/ppermute | solution.py:22
  69.7 7.5 %copy-start.22 = (s32[2,8]{1,0:T(2,128)S(1)}, s32[2,8]{1,0:T(2,128)}, u32[]{:S(2)}) copy-start(s32[2,8]{1,0:T(2,128)} %param.19) | copy-start | bytes 196
  69.7 25.9 %collective-permute-start.7 = (f32[256,1024]{1,0:T(8,128)}, f32[256,1024]{1,0:T(8,128)}, u32[]{:S(2)}, u32[]{:S(2)}) collective-permute-start(f32[256,1024]{1,0:T(8,128)} %pad_maximum_fusion.8), channel_id=1, source_target_pairs={{0,8},{4,12},{8,0},{12,4},{1,9},{5,13},{9,1},{13,5},{2,10},{6,14},... | collective-permute-start | bytes 3145736 | tf_op jit(solution)/shard_map/ppermute | solution.py:22
  71.5 55.1 %collective-permute-start.6 = (f32[256,1024]{1,0:T(8,128)}, f32[256,1024]{1,0:T(8,128)}, u32[]{:S(2)}, u32[]{:S(2)}) collective-permute-start(f32[256,1024]{1,0:T(8,128)} %pad_maximum_fusion.8), channel_id=1, source_target_pairs={{0,4},{4,0},{8,12},{12,8},{1,5},{5,1},{9,13},{13,9},{2,6},{6,2},{1... | collective-permute-start | bytes 3145736 | tf_op jit(solution)/shard_map/ppermute | solution.py:22
  77.4 4.4 %copy-start.11 = (f32[2,512,512]{2,1,0:T(8,128)S(1)}, f32[2,512,512]{2,1,0:T(8,128)}, u32[]{:S(2)}) copy-start(f32[2,512,512]{2,1,0:T(8,128)} %param.14) | copy-start | bytes 6291460
  95.6 31.0 %collective-permute-start.8 = (f32[256,1024]{1,0:T(8,128)}, f32[256,1024]{1,0:T(8,128)}, u32[]{:S(2)}, u32[]{:S(2)}) collective-permute-start(f32[256,1024]{1,0:T(8,128)} %collective-permute-done.7), channel_id=1, source_target_pairs={{0,4},{4,0},{8,12},{12,8},{1,5},{5,1},{9,13},{13,9},{2,6},{6,2},{1... | collective-permute-start | bytes 3145736 | tf_op jit(solution)/shard_map/ppermute | solution.py:22
  104.5 17.7 %copy-start.20 = (s32[2]{0:T(128)S(1)}, s32[2]{0:T(128)}, u32[]{:S(2)}) copy-start(s32[2]{0:T(128)} %param.16) | copy-start | bytes 28
  121.6 3.2 %collective-permute-start.4 = (f32[256]{0:T(256)S(1)}, f32[256]{0:T(256)S(1)}, u32[]{:S(2)}, u32[]{:S(2)}) collective-permute-start(f32[256]{0:T(256)S(1)} %get-tuple-element.42), channel_id=1, source_target_pairs={{0,4},{4,0},{8,12},{12,8},{1,5},{5,1},{9,13},{13,9},{2,6},{6,2},{1... | collective-permute-start | bytes 3080 | tf_op jit(solution)/shard_map/ppermute | solution.py:22
  124.7 6.3 %collective-permute-start.3 = (f32[256]{0:T(256)S(1)}, f32[256]{0:T(256)S(1)}, u32[]{:S(2)}, u32[]{:S(2)}) collective-permute-start(f32[256]{0:T(256)S(1)} %get-tuple-element.41), channel_id=1, source_target_pairs={{0,4},{4,0},{8,12},{12,8},{1,5},{5,1},{9,13},{13,9},{2,6},{6,2},{1... | collective-permute-start | bytes 3080 | tf_op jit(solution)/shard_map/ppermute | solution.py:22
  124.8 6.2 %collective-permute-start.5 = (f32[256]{0:T(256)S(1)}, f32[256]{0:T(256)S(1)}, u32[]{:S(2)}, u32[]{:S(2)}) collective-permute-start(f32[256]{0:T(256)S(1)} %slice_add_fusion.4), channel_id=1, source_target_pairs={{0,8},{4,12},{8,0},{12,4},{1,9},{5,13},{9,1},{13,5},{2,10},{6,14},... | collective-permute-start | bytes 3080 | tf_op jit(solution)/shard_map/ppermute | solution.py:22
  175.6 26.3 %collective-permute-start.16 = (f32[512,512]{1,0:T(8,128)}, f32[512,512]{1,0:T(8,128)}, u32[]{:S(2)}, u32[]{:S(2)}) collective-permute-start(f32[512,512]{1,0:T(8,128)} %fusion.69), channel_id=1, source_target_pairs={{0,8},{4,12},{8,0},{12,4},{1,9},{5,13},{9,1},{13,5},{2,10},{6,14},... | collective-permute-start | bytes 3145736 | tf_op jit(solution)/shard_map/ppermute | solution.py:22
  179.1 44.2 %copy-start.6 = (f32[512,512]{1,0:T(8,128)S(1)}, f32[512,512]{1,0:T(8,128)}, u32[]{:S(2)}) copy-start(f32[512,512]{1,0:T(8,128)} %fusion.92) | copy-start | bytes 3145732
  179.2 44.2 %copy-start.12 = (f32[512,512]{1,0:T(8,128)S(1)}, f32[512,512]{1,0:T(8,128)}, u32[]{:S(2)}) copy-start(f32[512,512]{1,0:T(8,128)} %get-tuple-element.12) | copy-start | bytes 3145732
  179.2 44.2 %copy-start.13 = (f32[512,512]{1,0:T(8,128)S(1)}, f32[512,512]{1,0:T(8,128)}, u32[]{:S(2)}) copy-start(f32[512,512]{1,0:T(8,128)} %get-tuple-element.13) | copy-start | bytes 3145732
  179.2 44.2 %copy-start.14 = (f32[512,512]{1,0:T(8,128)S(1)}, f32[512,512]{1,0:T(8,128)}, u32[]{:S(2)}) copy-start(f32[512,512]{1,0:T(8,128)} %get-tuple-element.14) | copy-start | bytes 3145732
  179.2 44.2 %copy-start.15 = (f32[512,512]{1,0:T(8,128)S(1)}, f32[512,512]{1,0:T(8,128)}, u32[]{:S(2)}) copy-start(f32[512,512]{1,0:T(8,128)} %get-tuple-element.15) | copy-start | bytes 3145732
  181.7 46.8 %slice-start = ((s8[8388608]{0:T(1024)(128)(4,1)}), s8[4194304]{0:T(1024)(128)(4,1)S(1)}, s32[]{:S(2)}) async-start(s8[8388608]{0:T(1024)(128)(4,1)} %bitcast.106), calls=%async_computation.2 | async-start | bytes 8388608
  186.0 42.6 %slice-start.1 = ((s8[8388608]{0:T(1024)(128)(4,1)}), s8[4194304]{0:T(1024)(128)(4,1)S(1)}, s32[]{:S(2)}) async-start(s8[8388608]{0:T(1024)(128)(4,1)} %bitcast.106), calls=%async_computation.3 | async-start | bytes 8388608
  186.0 37.4 %collective-permute-start.10 = (f32[512,512]{1,0:T(8,128)S(1)}, f32[512,512]{1,0:T(8,128)S(1)}, u32[]{:S(2)}, u32[]{:S(2)}) collective-permute-start(f32[512,512]{1,0:T(8,128)S(1)} %fusion.64), channel_id=1, source_target_pairs={{0,8},{4,12},{8,0},{12,4},{1,9},{5,13},{9,1},{13,5},{2,10},{6,14},... | collective-permute-start | bytes 3145736 | tf_op jit(solution)/shard_map/ppermute | solution.py:22
  186.6 36.8 %collective-permute-start.15 = (f32[512,512]{1,0:T(8,128)}, f32[512,512]{1,0:T(8,128)S(1)}, u32[]{:S(2)}, u32[]{:S(2)}) collective-permute-start(f32[512,512]{1,0:T(8,128)} %fusion.69), channel_id=1, source_target_pairs={{0,4},{4,0},{8,12},{12,8},{1,5},{5,1},{9,13},{13,9},{2,6},{6,2},{1... | collective-permute-start | bytes 3145736 | tf_op jit(solution)/shard_map/ppermute | solution.py:22
  201.9 21.5 %collective-permute-start.17 = (f32[512,512]{1,0:T(8,128)}, f32[512,512]{1,0:T(8,128)S(1)}, u32[]{:S(2)}, u32[]{:S(2)}) collective-permute-start(f32[512,512]{1,0:T(8,128)} %collective-permute-done.16), channel_id=1, source_target_pairs={{0,4},{4,0},{8,12},{12,8},{1,5},{5,1},{9,13},{13,9},{2,6},{6,2},{1... | collective-permute-start | bytes 3145736 | tf_op jit(solution)/shard_map/ppermute | solution.py:22
  201.9 30.0 %collective-permute-start.9 = (f32[512,512]{1,0:T(8,128)S(1)}, f32[512,512]{1,0:T(8,128)S(1)}, u32[]{:S(2)}, u32[]{:S(2)}) collective-permute-start(f32[512,512]{1,0:T(8,128)S(1)} %fusion.64), channel_id=1, source_target_pairs={{0,4},{4,0},{8,12},{12,8},{1,5},{5,1},{9,13},{13,9},{2,6},{6,2},{1... | collective-permute-start | bytes 3145736 | tf_op jit(solution)/shard_map/ppermute | solution.py:22
  223.4 8.6 %collective-permute-start.11 = (f32[512,512]{1,0:T(8,128)S(1)}, f32[512,512]{1,0:T(8,128)}, u32[]{:S(2)}, u32[]{:S(2)}) collective-permute-start(f32[512,512]{1,0:T(8,128)S(1)} %collective-permute-done.10), channel_id=1, source_target_pairs={{0,4},{4,0},{8,12},{12,8},{1,5},{5,1},{9,13},{13,9},{2,6},{6,2},{1... | collective-permute-start | bytes 3145736 | tf_op jit(solution)/shard_map/ppermute | solution.py:22
  228.5 8.4 %copy-start.7 = (f32[512,512]{1,0:T(8,128)}, f32[512,512]{1,0:T(8,128)S(1)}, u32[]{:S(2)}) copy-start(f32[512,512]{1,0:T(8,128)S(1)} %get-tuple-element.52) | copy-start | bytes 3145732
  230.4 10.1 %copy-start.4 = (f32[1024,512]{1,0:T(8,128)}, f32[1024,512]{1,0:T(8,128)S(1)}, u32[]{:S(2)}) copy-start(f32[1024,512]{1,0:T(8,128)S(1)} %fusion.40) | copy-start | bytes 6291460
  231.4 9.1 %collective-permute-start.19 = (f32[256,512]{1,0:T(8,128)S(1)}, f32[256,512]{1,0:T(8,128)S(1)}, u32[]{:S(2)}, u32[]{:S(2)}) collective-permute-start(f32[256,512]{1,0:T(8,128)S(1)} %get-tuple-element.22), channel_id=1, source_target_pairs={{0,4},{4,0},{8,12},{12,8},{1,5},{5,1},{9,13},{13,9},{2,6},{6,2},{1... | collective-permute-start | bytes 1572872 | tf_op jit(solution)/shard_map/ppermute | solution.py:22
  237.0 4.4 %copy-start.9 = (f32[512,512]{1,0:T(8,128)}, f32[512,512]{1,0:T(8,128)S(1)}, u32[]{:S(2)}) copy-start(f32[512,512]{1,0:T(8,128)S(1)} %get-tuple-element.56) | copy-start | bytes 3145732
  238.9 2.5 copy-start.5
  240.0 2.9 %collective-permute-start.13 = (f32[256,512]{1,0:T(8,128)}, f32[256,512]{1,0:T(8,128)}, u32[]{:S(2)}, u32[]{:S(2)}) collective-permute-start(f32[256,512]{1,0:T(8,128)} %get-tuple-element.20), channel_id=1, source_target_pairs={{0,4},{4,0},{8,12},{12,8},{1,5},{5,1},{9,13},{13,9},{2,6},{6,2},{1... | collective-permute-start | bytes 1572872 | tf_op jit(solution)/shard_map/ppermute | solution.py:22
  240.0 10.9 %collective-permute-start.18 = (f32[256,512]{1,0:T(8,128)}, f32[256,512]{1,0:T(8,128)}, u32[]{:S(2)}, u32[]{:S(2)}) collective-permute-start(f32[256,512]{1,0:T(8,128)} %get-tuple-element.21), channel_id=1, source_target_pairs={{0,4},{4,0},{8,12},{12,8},{1,5},{5,1},{9,13},{13,9},{2,6},{6,2},{1... | collective-permute-start | bytes 1572872 | tf_op jit(solution)/shard_map/ppermute | solution.py:22
  241.4 15.1 %collective-permute-start.20 = (f32[256,512]{1,0:T(8,128)}, f32[256,512]{1,0:T(8,128)}, u32[]{:S(2)}, u32[]{:S(2)}) collective-permute-start(f32[256,512]{1,0:T(8,128)} %slice_add_fusion), channel_id=1, source_target_pairs={{0,8},{4,12},{8,0},{12,4},{1,9},{5,13},{9,1},{13,5},{2,10},{6,14},... | collective-permute-start | bytes 1572872 | tf_op jit(solution)/shard_map/ppermute | solution.py:22
  242.9 17.1 %collective-permute-start.12 = (f32[256,512]{1,0:T(8,128)}, f32[256,512]{1,0:T(8,128)}, u32[]{:S(2)}, u32[]{:S(2)}) collective-permute-start(f32[256,512]{1,0:T(8,128)} %get-tuple-element.19), channel_id=1, source_target_pairs={{0,4},{4,0},{8,12},{12,8},{1,5},{5,1},{9,13},{13,9},{2,6},{6,2},{1... | collective-permute-start | bytes 1572872 | tf_op jit(solution)/shard_map/ppermute | solution.py:22
  244.9 21.8 %collective-permute-start.14 = (f32[256,512]{1,0:T(8,128)}, f32[256,512]{1,0:T(8,128)}, u32[]{:S(2)}, u32[]{:S(2)}) collective-permute-start(f32[256,512]{1,0:T(8,128)} %slice_add_fusion.2), channel_id=1, source_target_pairs={{0,8},{4,12},{8,0},{12,4},{1,9},{5,13},{9,1},{13,5},{2,10},{6,14},... | collective-permute-start | bytes 1572872 | tf_op jit(solution)/shard_map/ppermute | solution.py:22
  250.9 15.9 %copy-start.2 = (f32[1024,1024]{1,0:T(8,128)S(1)}, f32[1024,1024]{1,0:T(8,128)}, u32[]{:S(2)}) copy-start(f32[1024,1024]{1,0:T(8,128)} %pad_maximum_fusion.2) | copy-start | bytes 12582916
  259.9 10.1 %copy-start.8 = (f32[512,512]{1,0:T(8,128)S(1)}, f32[512,512]{1,0:T(8,128)}, u32[]{:S(2)}) copy-start(f32[512,512]{1,0:T(8,128)} %copy-done.7) | copy-start | bytes 3145732
  259.9 10.1 %copy-start.10 = (f32[512,512]{1,0:T(8,128)S(1)}, f32[512,512]{1,0:T(8,128)}, u32[]{:S(2)}) copy-start(f32[512,512]{1,0:T(8,128)} %copy-done.9) | copy-start | bytes 3145732
  266.8 9.4 %copy-start.1 = (f32[1,512,1024]{2,1,0:T(8,128)S(1)}, f32[1,512,1024]{2,1,0:T(8,128)}, u32[]{:S(2)}) copy-start(f32[1,512,1024]{2,1,0:T(8,128)} %param.11) | copy-start | bytes 6291460
  270.0 2.1 collective-permute-start.22
  271.6 3.0 %collective-permute-start.21 = (f32[2,128]{1,0:T(2,128)S(1)}, f32[2,128]{1,0:T(2,128)S(1)}, u32[]{:S(2)}, u32[]{:S(2)}) collective-permute-start(f32[2,128]{1,0:T(2,128)S(1)} %get-tuple-element.33), channel_id=1, source_target_pairs={{0,4},{4,0},{8,12},{12,8},{1,5},{5,1},{9,13},{13,9},{2,6},{6,2},{1... | collective-permute-start | bytes 3080 | tf_op jit(solution)/shard_map/ppermute | solution.py:22
  272.1 3.6 %collective-permute-start.23 = (f32[2,128]{1,0:T(2,128)S(1)}, f32[2,128]{1,0:T(2,128)S(1)}, u32[]{:S(2)}, u32[]{:S(2)}) collective-permute-start(f32[2,128]{1,0:T(2,128)S(1)} %fusion.146), channel_id=1, source_target_pairs={{0,8},{4,12},{8,0},{12,4},{1,9},{5,13},{9,1},{13,5},{2,10},{6,14},... | collective-permute-start | bytes 3080 | tf_op jit(solution)/shard_map/ppermute | solution.py:22
  (4 other events, 6.4 us)
Sparse Core Ops, SparseCore 0:
  17.9 152.3 all-gather.4
  171.8 78.9 all-gather.6

commit v3 on v2

--- a/solution.py
+++ b/solution.py
@@ -32,13 +32,15 @@
     return jnp.concatenate(pieces, axis)
 
 
-def row_blocks(block):
+def row_blocks(block, after=None):
     n = lax.axis_size("row")
     held = {0: block}
     bit = n // 2
     while bit:
         for d in sorted(held):
             held[d | bit] = swap(held[d], bit)
+            if after is not None and bit == n // 2:
+                held[d | bit], _ = lax.optimization_barrier((held[d | bit], after))
         bit //= 2
     return [held[d] for d in range(n)]
 
@@ -121,7 +123,7 @@
     block_r = []
     sums_j = []
     for i in range(nodes):
-        block_r.append(-product(root, jnp.concatenate(row_blocks(reduced[i]), 0)))
+        block_r.append(-product(root, jnp.concatenate(row_blocks(reduced[i], block_r[-1] if i else None), 0)))
         upper = crossed(parent_factor[i], block_r[i]).reshape(n, node_rows, width_two)
         sums_j.append(row_sum([upper[d] for d in range(n)]))
     block_j = []

time: 284 us -> 288 us (1.014)
  waiting for transfers between devices: 149 us -> 153 us
    ppermute x24, waiting for transfers between devices: 105 us -> 114 us  [swap(): return lax.ppermute(block, 'row', [(i, i ^ bit) for i in range(n)])]
    all_gather x1, waiting for transfers between devices: 4.88 us -> 0.21 us  [body(): all_grams = lax.all_gather(gram, 'col', axis=0)]
where the time goes in v3:
time: 288 us
  waiting for transfers between devices  153 us (53%)
  matrix products  65.3 us (23%)
  local copies, waits for them, and re-layouts  20.9 us (7%)
  between operations  18.5 us (6%)
  starting transfers between devices  16.4 us (6%)
  other arithmetic  14 us (5%)
    ppermute x24, waiting for transfers between devices, swap(): return lax.ppermute(block, 'row', [(i, i ^ bit) for i in range(n)])  114 us
    dot_general x12, matrix products, product(): jnp.dot(left, right, precision=PRECISION, preferred_element_type=jnp.floa...  56.1 us
    all_gather x1, waiting for transfers between devices, body(): all_factors = lax.all_gather(factor, 'col', axis=0)  38.6 us
    ppermute x24, starting transfers between devices, swap(): return lax.ppermute(block, 'row', [(i, i ^ bit) for i in range(n)])  16.1 us
    dot_general x3, matrix products, crossed(): lax.dot_general(left, right, (((0,), (0,)), ((), ())), precision=PRECISIO...  9.15 us
    slice x3, local copies, waits for them, and re-layouts, reordered(): block[:, (d ^ e) * share:((d ^ e) + 1) * share]  8.82 us
    dynamic_slice x2, local copies, waits for them, and re-layouts, own_first(): lax.dynamic_slice_in_dim(array, (me ^ d) * share, share, axis)  6.9 us
  transfers between devices with their start and end apart: 26, of which 9 were waited for; matrix products, arithmetic and copies ran while one was open for 30% of the time, Pallas kernels for 0%

profile of v3, /device:TPU:0, one launch (start us, length us, event | category | flops | bytes accessed | tf_op | source)
XLA Modules:
  0.0 287.7 jit_solution(6290509429830668163)
XLA Ops:
  7.3 1.5 multiply_reduce_fusion.4
  8.8 2.5 dynamic-slice_bitcast_fusion.2
  11.3 0.9 copy-done.17
  12.9 4.8 %fusion.59 = f32[512,1024]{1,0:T(8,128)} fusion(f32[1,512,1024]{2,1,0:T(8,128)S(1)} %copy-done, f32[1024,256]{1,0:T(8,128)S(1)} %get-tuple-element.19, f32[1024,256]{1,0:T(8,128)S(1)} %get-tuple-element.20, f32[1024,256]{1,0:T(8,128)S(1)} %get-tuple-element.18, f32[1024,256]{1,0:T(8,128)S(1)} %get-tuple-element.13), kind=kOutput, calls=%fused_computation.65 | convolution fusion | flops 3224371200 | bytes 8388608 | tf_op jit(solution)/shard_map/dot_general | solution.py:11
  18.0 3.0 %collective-permute-start.1 = (f32[512,1024]{1,0:T(8,128)}, f32[512,1024]{1,0:T(8,128)}, u32[]{:S(2)}, u32[]{:S(2)}) collective-permute-start(f32[512,1024]{1,0:T(8,128)} %fusion.59), channel_id=1, source_target_pairs={{0,8},{4,12},{8,0},{12,4},{1,9},{5,13},{9,1},{13,5},{2,10},{6,14},... | collective-permute-start | bytes 6291464 | tf_op jit(solution)/shard_map/ppermute | solution.py:22
  21.5 2.0 fusion.102
  23.5 43.5 %collective-permute-done.1 = f32[512,1024]{1,0:T(8,128)} collective-permute-done((f32[512,1024]{1,0:T(8,128)}, f32[512,1024]{1,0:T(8,128)}, u32[]{:S(2)}, u32[]{:S(2)}) %collective-permute-start.1) | collective-permute-done | bytes 2097184 | tf_op jit(solution)/shard_map/ppermute | solution.py:22
  67.0 1.7 fusion.98
  68.7 1.1 pad_maximum_fusion.8
  69.7 1.7 collective-permute-start.7
  71.7 5.4 %fusion.38 = f32[256,1024]{1,0:T(8,128)} fusion(f32[1024,256]{1,0:T(8,128)} %copy-done.16, f32[1024,256]{1,0:T(8,128)} %copy-done.18, f32[1024,256]{1,0:T(8,128)} %copy-done.19, f32[1024,256]{1,0:T(8,128)} %copy-done.17), kind=kOutput, calls=%fused_computation.41 | convolution fusion | flops 1613758464 | bytes 5242880 | tf_op jit(solution)/shard_map/dot_general | solution.py:15
  77.4 4.4 %constant_dynamic-slice_fusion.13 = (f32[512,512]{1,0:T(8,128)}, f32[512,512]{1,0:T(8,128)}, f32[512,512]{1,0:T(8,128)}, f32[512,512]{1,0:T(8,128)}) fusion(f32[512,2048]{1,0:T(8,128)} %param.10, s32[]{:T(128)S(6)} %select_n.52, s32[]{:T(128)S(6)} %select_n.53, s32[]{:T(128)S(6)} %select_n.55, s32[]{:T(128)S(6)} %select_n.54), kind=kLoop, calls=%fused_computation.151 | loop fusion | bytes 8388624 | tf_op jit(solution)/shard_map/dynamic_slice | solution.py:30
  81.8 2.0 fusion.95
  83.9 11.8 %collective-permute-done.7 = f32[256,1024]{1,0:T(8,128)} collective-permute-done((f32[256,1024]{1,0:T(8,128)}, f32[256,1024]{1,0:T(8,128)}, u32[]{:S(2)}, u32[]{:S(2)}) %collective-permute-start.7) | collective-permute-done | bytes 1048608 | tf_op jit(solution)/shard_map/ppermute | solution.py:22
  95.6 2.9 %fusion.156 = (f32[512,256]{1,0:T(8,128)}, f32[512,256]{1,0:T(8,128)}, f32[512,256]{1,0:T(8,128)}, f32[512,256]{1,0:T(8,128)}) fusion(f32[512,1024]{1,0:T(8,128)} %collective-permute-done), kind=kLoop, calls=%fused_computation.179 | loop fusion | bytes 4194304 | tf_op jit(solution)/shard_map/slice | solution.py:63
  98.5 3.1 %fusion.157 = (f32[512,512]{1,0:T(8,128)}, f32[512,512]{1,0:T(8,128)}) fusion(f32[512,1024]{1,0:T(8,128)} %collective-permute-done.1), kind=kLoop, calls=%fused_computation.180 | loop fusion | bytes 4194304 | tf_op jit(solution)/shard_map/slice | solution.py:63
  101.6 2.9 %fusion.158 = (f32[512,256]{1,0:T(8,128)}, f32[512,256]{1,0:T(8,128)}, f32[512,256]{1,0:T(8,128)}, f32[512,256]{1,0:T(8,128)}) fusion(f32[512,1024]{1,0:T(8,128)} %collective-permute-done.2), kind=kLoop, calls=%fused_computation.181 | loop fusion | bytes 4194304 | tf_op jit(solution)/shard_map/slice | solution.py:63
  104.5 17.1 %multiply_reduce_fusion.1 = f32[1024]{0:T(1024)S(1)} fusion(f32[512,1024]{1,0:T(8,128)} %fusion.59, f32[512,256]{1,0:T(8,128)} %get-tuple-element.32, f32[512,256]{1,0:T(8,128)} %get-tuple-element.33, f32[512,256]{1,0:T(8,128)} %get-tuple-element.34, f32[512,256]{1,0:T(8,128)} %get-tuple-element.31, f32[512,512]{1,0:T(8,128)} %get-tuple-element.30, ...), kind=kOutput, calls=%fused_computation.54 | convolution fusion | flops 6467615744 | bytes 12587008 | tf_op jit(solution)/shard_map/dot_general | solution.py:11
  122.2 0.7 fusion.161
  124.9 1.8 collective-permute-start.5
  126.7 4.4 %pad_maximum_fusion.2 = f32[1024,1024]{1,0:T(8,128)} fusion(f32[256,1024]{1,0:T(8,128)} %collective-permute-done.8, f32[256,1024]{1,0:T(8,128)} %collective-permute-done.7, f32[256,1024]{1,0:T(8,128)} %collective-permute-done.6, f32[256,512]{1,0:T(8,128)S(1)} %fusion.98, f32[256,512]{1,0:T(8,128)S(1)} %fusion.102), kind=kLoop, calls=%fused_computation.24 | loop fusion | flops 4194304 | bytes 8388608 | tf_op jit(solution)/shard_map/concatenate | solution.py:103
  131.1 0.6 add_add_fusion
  131.7 38.6 %all-gather.5.cloned.1.call-done = f32[2048,1024]{1,0:T(8,128)} async-done(((f32[512,1024]{1,0:T(8,128)}), f32[2048,1024]{1,0:T(8,128)}) %all-gather.5.cloned.1.call-update) | async-done | bytes 8388624 | tf_op jit(solution)/shard_map/all_gather | solution.py:87
  170.3 5.3 %fusion.64 = f32[512,512]{1,0:T(8,128)} fusion(f32[512,512]{1,0:T(8,128)} %fusion.95, f32[1024,1024]{1,0:T(8,128)} %pad_maximum_fusion.2, f32[4,512,1024]{2,1,0:T(8,128)} %bitcast.104, s32[]{:T(128)S(6)} %select_n.57), kind=kOutput, calls=%fused_computation.66 | convolution fusion | flops 1610874880 | bytes 6291460 | tf_op jit(solution)/shard_map/dot_general | solution.py:11
  175.6 1.5 collective-permute-start.10
  179.4 21.6 %collective-permute-done.10 = f32[512,512]{1,0:T(8,128)} collective-permute-done((f32[512,512]{1,0:T(8,128)}, f32[512,512]{1,0:T(8,128)}, u32[]{:S(2)}, u32[]{:S(2)}) %collective-permute-start.10) | collective-permute-done | bytes 1048608 | tf_op jit(solution)/shard_map/ppermute | solution.py:22
  201.0 2.3 fusion.92
  203.3 4.2 %fusion.69 = f32[512,512]{1,0:T(8,128)S(1)} fusion(f32[512,512]{1,0:T(8,128)S(1)} %fusion.92, f32[1024,1024]{1,0:T(8,128)} %pad_maximum_fusion.2, f32[4,512,1024]{2,1,0:T(8,128)} %bitcast.105, s32[]{:T(128)S(6)} %select_n.58), kind=kOutput, calls=%fused_computation.67 | convolution fusion | flops 1610874880 | bytes 6291460 | tf_op jit(solution)/shard_map/dot_general | solution.py:11
  207.5 1.5 collective-permute-start.16
  209.3 5.1 %multiply_reduce_fusion.3 = (f32[512]{0:T(512)S(1)}, f32[512,512]{1,0:T(8,128)S(1)}) fusion(f32[512,512]{1,0:T(8,128)S(1)} %copy-done.6, f32[512,512]{1,0:T(8,128)S(1)} %collective-permute-done.11, f32[512,512]{1,0:T(8,128)} %collective-permute-done.10, f32[512,512]{1,0:T(8,128)S(1)} %collective-permute-done.9, f32[512,512]{1,0:T(8,128)} %fusion.64, ...), kind=kOutput, calls=%fused_computation.93 | convolution fusion | flops 3228302848 | bytes 10487808 | tf_op jit(solution)/shard_map/dot_general | solution.py:11
  214.4 18.7 %collective-permute-done.16 = f32[512,512]{1,0:T(8,128)S(1)} collective-permute-done((f32[512,512]{1,0:T(8,128)S(1)}, f32[512,512]{1,0:T(8,128)S(1)}, u32[]{:S(2)}, u32[]{:S(2)}) %collective-permute-start.16) | collective-permute-done | bytes 1048608 | tf_op jit(solution)/shard_map/ppermute | solution.py:22
  233.2 1.8 fusion.44
  235.1 1.0 fusion.154
  236.5 5.1 %multiply_reduce_fusion.2 = (f32[512]{0:T(512)S(1)}, f32[512,512]{1,0:T(8,128)S(1)}) fusion(f32[512,512]{1,0:T(8,128)S(1)} %fusion.92, f32[512,512]{1,0:T(8,128)} %collective-permute-done.17, f32[512,512]{1,0:T(8,128)S(1)} %collective-permute-done.16, f32[512,512]{1,0:T(8,128)S(1)} %collective-permute-done.15, f32[512,512]{1,0:T(8,128)S(1)} %fusion.69, ...), kind=kOutput, calls=%fused_computation.88 | convolution fusion | flops 3228302848 | bytes 10487808 | tf_op jit(solution)/shard_map/dot_general | solution.py:11
  241.6 1.8 fusion.40
  243.5 1.1 fusion.155
  245.2 0.9 slice_add_fusion.2
  246.0 1.5 collective-permute-start.14
  247.5 2.1 slice_add_fusion
  249.6 0.8 collective-permute-start.20
  250.9 10.3 %collective-permute-done.14 = f32[256,512]{1,0:T(8,128)} collective-permute-done((f32[256,512]{1,0:T(8,128)}, f32[256,512]{1,0:T(8,128)}, u32[]{:S(2)}, u32[]{:S(2)}) %collective-permute-start.14) | collective-permute-done | bytes 524320 | tf_op jit(solution)/shard_map/ppermute | solution.py:22
  261.1 3.4 %multiply_reduce_fusion.6 = (f32[512]{0:T(512)S(1)}, f32[256,512]{1,0:T(8,128)S(1)}) fusion(f32[256,512]{1,0:T(8,128)S(1)} %fusion.102, f32[256,512]{1,0:T(8,128)} %collective-permute-done.14, f32[256,512]{1,0:T(8,128)} %collective-permute-done.12, f32[1024,512]{1,0:T(8,128)} %copy-done.4, f32[1024,1024]{1,0:T(8,128)} %pad_maximum_fusion.2, ...), kind=kOutput, calls=%fused_computation.118 | convolution fusion | flops 806092288 | bytes 5769220 | tf_op jit(solution)/shard_map/dot_general | solution.py:11
  264.6 6.8 %collective-permute-done.20 = f32[256,512]{1,0:T(8,128)} collective-permute-done((f32[256,512]{1,0:T(8,128)}, f32[256,512]{1,0:T(8,128)}, u32[]{:S(2)}, u32[]{:S(2)}) %collective-permute-start.20) | collective-permute-done | bytes 524320 | tf_op jit(solution)/shard_map/ppermute | solution.py:22
  271.4 3.1 %multiply_reduce_fusion.5 = (f32[512]{0:T(512)S(1)}, f32[256,512]{1,0:T(8,128)S(1)}) fusion(f32[256,512]{1,0:T(8,128)S(1)} %fusion.98, f32[256,512]{1,0:T(8,128)} %collective-permute-done.20, f32[256,512]{1,0:T(8,128)} %collective-permute-done.18, f32[1024,512]{1,0:T(8,128)} %copy-done.5, f32[1024,1024]{1,0:T(8,128)S(1)} %copy-done.2, ...), kind=kOutput, calls=%fused_computation.115 | convolution fusion | flops 806092288 | bytes 5769220 | tf_op jit(solution)/shard_map/dot_general | solution.py:11
  274.7 1.5 pad_maximum_fusion.5
  276.7 1.5 collective-permute-start.23
  278.2 1.0 pad_maximum_fusion.9
  279.2 1.1 collective-permute-done.23
  (114 shorter events, 5.7 us)
Async XLA Ops:
  7.2 5.8 %copy-start = (f32[1,512,1024]{2,1,0:T(8,128)S(1)}, f32[1,512,1024]{2,1,0:T(8,128)}, u32[]{:S(2)}) copy-start(f32[1,512,1024]{2,1,0:T(8,128)} %param.11) | copy-start | bytes 6291460
  7.2 163.1 %all-gather.5.cloned.1.call-start = ((), (), s32[]{:S(2)}) async-start(), calls=%async_computation | async-start | bytes 10485760 | tf_op jit(solution)/shard_map/all_gather | solution.py:87
  12.9 8.1 %copy-start.21 = (s32[2,4]{1,0:T(2,128)S(1)}, s32[2,4]{1,0:T(2,128)}, u32[]{:S(2)}) copy-start(s32[2,4]{1,0:T(2,128)} %param.18) | copy-start | bytes 100
  12.9 8.1 %copy-start.23 = (s32[2]{0:T(128)S(1)}, s32[2]{0:T(128)}, u32[]{:S(2)}) copy-start(s32[2]{0:T(128)} %param.17) | copy-start | bytes 28
  17.8 49.2 %copy-start.3 = (f32[2,512,512]{2,1,0:T(8,128)S(1)}, f32[2,512,512]{2,1,0:T(8,128)}, u32[]{:S(2)}) copy-start(f32[2,512,512]{2,1,0:T(8,128)} %param.15) | copy-start | bytes 6291460
  17.8 233.1 %all-gather.7.cloned.1.call-start = ((), (), s32[]{:S(2)}) async-start(), calls=%async_computation.1 | async-start | bytes 5242880 | tf_op jit(solution)/shard_map/all_gather | solution.py:90
  18.0 49.0 %collective-permute-start.1 = (f32[512,1024]{1,0:T(8,128)}, f32[512,1024]{1,0:T(8,128)}, u32[]{:S(2)}, u32[]{:S(2)}) collective-permute-start(f32[512,1024]{1,0:T(8,128)} %fusion.59), channel_id=1, source_target_pairs={{0,8},{4,12},{8,0},{12,4},{1,9},{5,13},{9,1},{13,5},{2,10},{6,14},... | collective-permute-start | bytes 6291464 | tf_op jit(solution)/shard_map/ppermute | solution.py:22
  21.0 74.6 %collective-permute-start = (f32[512,1024]{1,0:T(8,128)}, f32[512,1024]{1,0:T(8,128)}, u32[]{:S(2)}, u32[]{:S(2)}) collective-permute-start(f32[512,1024]{1,0:T(8,128)} %fusion.59), channel_id=1, source_target_pairs={{0,4},{4,0},{8,12},{12,8},{1,5},{5,1},{9,13},{13,9},{2,6},{6,2},{1... | collective-permute-start | bytes 6291464 | tf_op jit(solution)/shard_map/ppermute | solution.py:22
  67.0 34.6 %collective-permute-start.2 = (f32[512,1024]{1,0:T(8,128)}, f32[512,1024]{1,0:T(8,128)}, u32[]{:S(2)}, u32[]{:S(2)}) collective-permute-start(f32[512,1024]{1,0:T(8,128)} %collective-permute-done.1), channel_id=1, source_target_pairs={{0,4},{4,0},{8,12},{12,8},{1,5},{5,1},{9,13},{13,9},{2,6},{6,2},{1... | collective-permute-start | bytes 6291464 | tf_op jit(solution)/shard_map/ppermute | solution.py:22
  69.7 7.5 %copy-start.22 = (s32[2,8]{1,0:T(2,128)S(1)}, s32[2,8]{1,0:T(2,128)}, u32[]{:S(2)}) copy-start(s32[2,8]{1,0:T(2,128)} %param.19) | copy-start | bytes 196
  69.7 25.9 %collective-permute-start.7 = (f32[256,1024]{1,0:T(8,128)}, f32[256,1024]{1,0:T(8,128)}, u32[]{:S(2)}, u32[]{:S(2)}) collective-permute-start(f32[256,1024]{1,0:T(8,128)} %pad_maximum_fusion.8), channel_id=1, source_target_pairs={{0,8},{4,12},{8,0},{12,4},{1,9},{5,13},{9,1},{13,5},{2,10},{6,14},... | collective-permute-start | bytes 3145736 | tf_op jit(solution)/shard_map/ppermute | solution.py:22
  71.5 55.2 %collective-permute-start.6 = (f32[256,1024]{1,0:T(8,128)}, f32[256,1024]{1,0:T(8,128)}, u32[]{:S(2)}, u32[]{:S(2)}) collective-permute-start(f32[256,1024]{1,0:T(8,128)} %pad_maximum_fusion.8), channel_id=1, source_target_pairs={{0,4},{4,0},{8,12},{12,8},{1,5},{5,1},{9,13},{13,9},{2,6},{6,2},{1... | collective-permute-start | bytes 3145736 | tf_op jit(solution)/shard_map/ppermute | solution.py:22
  77.4 4.4 %copy-start.11 = (f32[2,512,512]{2,1,0:T(8,128)S(1)}, f32[2,512,512]{2,1,0:T(8,128)}, u32[]{:S(2)}) copy-start(f32[2,512,512]{2,1,0:T(8,128)} %param.14) | copy-start | bytes 6291460
  95.6 31.1 %collective-permute-start.8 = (f32[256,1024]{1,0:T(8,128)}, f32[256,1024]{1,0:T(8,128)}, u32[]{:S(2)}, u32[]{:S(2)}) collective-permute-start(f32[256,1024]{1,0:T(8,128)} %collective-permute-done.7), channel_id=1, source_target_pairs={{0,4},{4,0},{8,12},{12,8},{1,5},{5,1},{9,13},{13,9},{2,6},{6,2},{1... | collective-permute-start | bytes 3145736 | tf_op jit(solution)/shard_map/ppermute | solution.py:22
  104.5 17.7 %copy-start.20 = (s32[2]{0:T(128)S(1)}, s32[2]{0:T(128)}, u32[]{:S(2)}) copy-start(s32[2]{0:T(128)} %param.16) | copy-start | bytes 28
  121.6 3.3 %collective-permute-start.4 = (f32[256]{0:T(256)S(1)}, f32[256]{0:T(256)S(1)}, u32[]{:S(2)}, u32[]{:S(2)}) collective-permute-start(f32[256]{0:T(256)S(1)} %get-tuple-element.44), channel_id=1, source_target_pairs={{0,4},{4,0},{8,12},{12,8},{1,5},{5,1},{9,13},{13,9},{2,6},{6,2},{1... | collective-permute-start | bytes 3080 | tf_op jit(solution)/shard_map/ppermute | solution.py:22
  124.8 6.3 %collective-permute-start.3 = (f32[256]{0:T(256)S(1)}, f32[256]{0:T(256)S(1)}, u32[]{:S(2)}, u32[]{:S(2)}) collective-permute-start(f32[256]{0:T(256)S(1)} %get-tuple-element.43), channel_id=1, source_target_pairs={{0,4},{4,0},{8,12},{12,8},{1,5},{5,1},{9,13},{13,9},{2,6},{6,2},{1... | collective-permute-start | bytes 3080 | tf_op jit(solution)/shard_map/ppermute | solution.py:22
  124.9 6.2 %collective-permute-start.5 = (f32[256]{0:T(256)S(1)}, f32[256]{0:T(256)S(1)}, u32[]{:S(2)}, u32[]{:S(2)}) collective-permute-start(f32[256]{0:T(256)S(1)} %slice_add_fusion.4), channel_id=1, source_target_pairs={{0,8},{4,12},{8,0},{12,4},{1,9},{5,13},{9,1},{13,5},{2,10},{6,14},... | collective-permute-start | bytes 3080 | tf_op jit(solution)/shard_map/ppermute | solution.py:22
  175.6 25.4 %collective-permute-start.10 = (f32[512,512]{1,0:T(8,128)}, f32[512,512]{1,0:T(8,128)}, u32[]{:S(2)}, u32[]{:S(2)}) collective-permute-start(f32[512,512]{1,0:T(8,128)} %fusion.64), channel_id=1, source_target_pairs={{0,8},{4,12},{8,0},{12,4},{1,9},{5,13},{9,1},{13,5},{2,10},{6,14},... | collective-permute-start | bytes 3145736 | tf_op jit(solution)/shard_map/ppermute | solution.py:22
  179.3 30.0 %copy-start.6 = (f32[512,512]{1,0:T(8,128)S(1)}, f32[512,512]{1,0:T(8,128)}, u32[]{:S(2)}) copy-start(f32[512,512]{1,0:T(8,128)} %fusion.95) | copy-start | bytes 3145732
  179.3 30.0 %copy-start.12 = (f32[512,512]{1,0:T(8,128)S(1)}, f32[512,512]{1,0:T(8,128)}, u32[]{:S(2)}) copy-start(f32[512,512]{1,0:T(8,128)} %get-tuple-element.14) | copy-start | bytes 3145732
  179.3 30.0 %copy-start.13 = (f32[512,512]{1,0:T(8,128)S(1)}, f32[512,512]{1,0:T(8,128)}, u32[]{:S(2)}) copy-start(f32[512,512]{1,0:T(8,128)} %get-tuple-element.15) | copy-start | bytes 3145732
  179.3 30.0 %copy-start.14 = (f32[512,512]{1,0:T(8,128)S(1)}, f32[512,512]{1,0:T(8,128)}, u32[]{:S(2)}) copy-start(f32[512,512]{1,0:T(8,128)} %get-tuple-element.16) | copy-start | bytes 3145732
  179.3 30.0 %copy-start.15 = (f32[512,512]{1,0:T(8,128)S(1)}, f32[512,512]{1,0:T(8,128)}, u32[]{:S(2)}) copy-start(f32[512,512]{1,0:T(8,128)} %get-tuple-element.17) | copy-start | bytes 3145732
  179.3 30.0 %collective-permute-start.9 = (f32[512,512]{1,0:T(8,128)}, f32[512,512]{1,0:T(8,128)S(1)}, u32[]{:S(2)}, u32[]{:S(2)}) collective-permute-start(f32[512,512]{1,0:T(8,128)} %fusion.64), channel_id=1, source_target_pairs={{0,4},{4,0},{8,12},{12,8},{1,5},{5,1},{9,13},{13,9},{2,6},{6,2},{1... | collective-permute-start | bytes 3145736 | tf_op jit(solution)/shard_map/ppermute | solution.py:22
  201.0 8.3 %collective-permute-start.11 = (f32[512,512]{1,0:T(8,128)}, f32[512,512]{1,0:T(8,128)S(1)}, u32[]{:S(2)}, u32[]{:S(2)}) collective-permute-start(f32[512,512]{1,0:T(8,128)} %collective-permute-done.10), channel_id=1, source_target_pairs={{0,4},{4,0},{8,12},{12,8},{1,5},{5,1},{9,13},{13,9},{2,6},{6,2},{1... | collective-permute-start | bytes 3145736 | tf_op jit(solution)/shard_map/ppermute | solution.py:22
  203.3 29.9 %slice-start = ((s8[8388608]{0:T(1024)(128)(4,1)}), s8[4194304]{0:T(1024)(128)(4,1)S(1)}, s32[]{:S(2)}) async-start(s8[8388608]{0:T(1024)(128)(4,1)} %bitcast.106), calls=%async_computation.2 | async-start | bytes 8388608
  207.5 25.7 %slice-start.1 = ((s8[8388608]{0:T(1024)(128)(4,1)}), s8[4194304]{0:T(1024)(128)(4,1)S(1)}, s32[]{:S(2)}) async-start(s8[8388608]{0:T(1024)(128)(4,1)} %bitcast.106), calls=%async_computation.3 | async-start | bytes 8388608
  207.5 25.6 %collective-permute-start.16 = (f32[512,512]{1,0:T(8,128)S(1)}, f32[512,512]{1,0:T(8,128)S(1)}, u32[]{:S(2)}, u32[]{:S(2)}) collective-permute-start(f32[512,512]{1,0:T(8,128)S(1)} %fusion.69), channel_id=1, source_target_pairs={{0,8},{4,12},{8,0},{12,4},{1,9},{5,13},{9,1},{13,5},{2,10},{6,14},... | collective-permute-start | bytes 3145736 | tf_op jit(solution)/shard_map/ppermute | solution.py:22
  209.1 27.5 %collective-permute-start.15 = (f32[512,512]{1,0:T(8,128)S(1)}, f32[512,512]{1,0:T(8,128)S(1)}, u32[]{:S(2)}, u32[]{:S(2)}) collective-permute-start(f32[512,512]{1,0:T(8,128)S(1)} %fusion.69), channel_id=1, source_target_pairs={{0,4},{4,0},{8,12},{12,8},{1,5},{5,1},{9,13},{13,9},{2,6},{6,2},{1... | collective-permute-start | bytes 3145736 | tf_op jit(solution)/shard_map/ppermute | solution.py:22
  214.4 27.2 %copy-start.7 = (f32[512,512]{1,0:T(8,128)}, f32[512,512]{1,0:T(8,128)S(1)}, u32[]{:S(2)}) copy-start(f32[512,512]{1,0:T(8,128)S(1)} %get-tuple-element.58) | copy-start | bytes 3145732
  233.2 3.4 %collective-permute-start.17 = (f32[512,512]{1,0:T(8,128)S(1)}, f32[512,512]{1,0:T(8,128)}, u32[]{:S(2)}, u32[]{:S(2)}) collective-permute-start(f32[512,512]{1,0:T(8,128)S(1)} %collective-permute-done.16), channel_id=1, source_target_pairs={{0,4},{4,0},{8,12},{12,8},{1,5},{5,1},{9,13},{13,9},{2,6},{6,2},{1... | collective-permute-start | bytes 3145736 | tf_op jit(solution)/shard_map/ppermute | solution.py:22
  235.0 10.1 %copy-start.4 = (f32[1024,512]{1,0:T(8,128)}, f32[1024,512]{1,0:T(8,128)S(1)}, u32[]{:S(2)}) copy-start(f32[1024,512]{1,0:T(8,128)S(1)} %fusion.44) | copy-start | bytes 6291460
  236.0 9.1 %collective-permute-start.13 = (f32[256,512]{1,0:T(8,128)S(1)}, f32[256,512]{1,0:T(8,128)S(1)}, u32[]{:S(2)}, u32[]{:S(2)}) collective-permute-start(f32[256,512]{1,0:T(8,128)S(1)} %get-tuple-element.22), channel_id=1, source_target_pairs={{0,4},{4,0},{8,12},{12,8},{1,5},{5,1},{9,13},{13,9},{2,6},{6,2},{1... | collective-permute-start | bytes 1572872 | tf_op jit(solution)/shard_map/ppermute | solution.py:22
  241.6 4.4 %copy-start.9 = (f32[512,512]{1,0:T(8,128)}, f32[512,512]{1,0:T(8,128)S(1)}, u32[]{:S(2)}) copy-start(f32[512,512]{1,0:T(8,128)S(1)} %get-tuple-element.54) | copy-start | bytes 3145732
  243.5 2.6 copy-start.5
  244.6 2.9 collective-permute-start.19
  244.7 6.2 %collective-permute-start.12 = (f32[256,512]{1,0:T(8,128)}, f32[256,512]{1,0:T(8,128)}, u32[]{:S(2)}, u32[]{:S(2)}) collective-permute-start(f32[256,512]{1,0:T(8,128)} %get-tuple-element.21), channel_id=1, source_target_pairs={{0,4},{4,0},{8,12},{12,8},{1,5},{5,1},{9,13},{13,9},{2,6},{6,2},{1... | collective-permute-start | bytes 1572872 | tf_op jit(solution)/shard_map/ppermute | solution.py:22
  246.0 15.1 %collective-permute-start.14 = (f32[256,512]{1,0:T(8,128)}, f32[256,512]{1,0:T(8,128)}, u32[]{:S(2)}, u32[]{:S(2)}) collective-permute-start(f32[256,512]{1,0:T(8,128)} %slice_add_fusion.2), channel_id=1, source_target_pairs={{0,8},{4,12},{8,0},{12,4},{1,9},{5,13},{9,1},{13,5},{2,10},{6,14},... | collective-permute-start | bytes 1572872 | tf_op jit(solution)/shard_map/ppermute | solution.py:22
  247.5 17.1 %collective-permute-start.18 = (f32[256,512]{1,0:T(8,128)}, f32[256,512]{1,0:T(8,128)}, u32[]{:S(2)}, u32[]{:S(2)}) collective-permute-start(f32[256,512]{1,0:T(8,128)} %get-tuple-element.23), channel_id=1, source_target_pairs={{0,4},{4,0},{8,12},{12,8},{1,5},{5,1},{9,13},{13,9},{2,6},{6,2},{1... | collective-permute-start | bytes 1572872 | tf_op jit(solution)/shard_map/ppermute | solution.py:22
  249.6 21.8 %collective-permute-start.20 = (f32[256,512]{1,0:T(8,128)}, f32[256,512]{1,0:T(8,128)}, u32[]{:S(2)}, u32[]{:S(2)}) collective-permute-start(f32[256,512]{1,0:T(8,128)} %slice_add_fusion), channel_id=1, source_target_pairs={{0,8},{4,12},{8,0},{12,4},{1,9},{5,13},{9,1},{13,5},{2,10},{6,14},... | collective-permute-start | bytes 1572872 | tf_op jit(solution)/shard_map/ppermute | solution.py:22
  250.9 20.6 %copy-start.2 = (f32[1024,1024]{1,0:T(8,128)S(1)}, f32[1024,1024]{1,0:T(8,128)}, u32[]{:S(2)}) copy-start(f32[1024,1024]{1,0:T(8,128)} %pad_maximum_fusion.2) | copy-start | bytes 12582916
  264.6 10.1 %copy-start.8 = (f32[512,512]{1,0:T(8,128)S(1)}, f32[512,512]{1,0:T(8,128)}, u32[]{:S(2)}) copy-start(f32[512,512]{1,0:T(8,128)} %copy-done.7) | copy-start | bytes 3145732
  264.6 10.1 %copy-start.10 = (f32[512,512]{1,0:T(8,128)S(1)}, f32[512,512]{1,0:T(8,128)}, u32[]{:S(2)}) copy-start(f32[512,512]{1,0:T(8,128)} %copy-done.9) | copy-start | bytes 3145732
  271.4 9.4 %copy-start.1 = (f32[1,512,1024]{2,1,0:T(8,128)S(1)}, f32[1,512,1024]{2,1,0:T(8,128)}, u32[]{:S(2)}) copy-start(f32[1,512,1024]{2,1,0:T(8,128)} %param.11) | copy-start | bytes 6291460
  274.6 2.1 collective-permute-start.22
  276.2 3.0 %collective-permute-start.21 = (f32[2,128]{1,0:T(2,128)S(1)}, f32[2,128]{1,0:T(2,128)S(1)}, u32[]{:S(2)}, u32[]{:S(2)}) collective-permute-start(f32[2,128]{1,0:T(2,128)S(1)} %get-tuple-element.35), channel_id=1, source_target_pairs={{0,4},{4,0},{8,12},{12,8},{1,5},{5,1},{9,13},{13,9},{2,6},{6,2},{1... | collective-permute-start | bytes 3080 | tf_op jit(solution)/shard_map/ppermute | solution.py:22
  276.7 3.6 %collective-permute-start.23 = (f32[2,128]{1,0:T(2,128)S(1)}, f32[2,128]{1,0:T(2,128)S(1)}, u32[]{:S(2)}, u32[]{:S(2)}) collective-permute-start(f32[2,128]{1,0:T(2,128)S(1)} %fusion.146), channel_id=1, source_target_pairs={{0,8},{4,12},{8,0},{12,4},{1,9},{5,13},{9,1},{13,5},{2,10},{6,14},... | collective-permute-start | bytes 3080 | tf_op jit(solution)/shard_map/ppermute | solution.py:22
  (4 other events, 6.4 us)
Sparse Core Ops, SparseCore 0:
  17.9 152.3 all-gather.4
  171.8 78.9 all-gather.6
